TPU v7x, 256 devices: a whole 4x4x8 slice. The times are simulated.
256 devices in a mesh: scen: 32 (over y, x, core), fac: 8 (over z).
Axes of the slice: x: 4, y: 4, z: 8, core: 2. Of those that a mesh axis runs over, the one named last changes fastest.
Arguments:
- duals: bfloat16 [256, 4096, 128], P('scen', 'fac'), may hold values from -48 to 48
- tiles: bfloat16 [256, 1024, 4096], P('scen', 'fac'), may hold values from -0.5 to 0.5
- tile_rows: int32 [256, 1024], P('scen', 'fac'), may hold values from 0 to 7
- tile_cols: int32 [256, 1024], P('scen', 'fac'), may hold values from 0 to 39
- block_counts: int32 [256, 8], P('scen', 'fac'), may hold values from 32 to 128, as said below
- probabilities: float32 [256], P('scen'), may hold values from 0.001171875 to 0.01171875
- customer_map: int32 [64], replicated, may hold values from 0 to 7, as said below
- costs: float32 [20480, 128], P('fac'), may hold values from -6 to 6
Outputs:
- reduced: float32 [20480, 128], P('fac')
Inputs may be any that keep to these rules, and one draw needn't show every extreme that they name: `customer_map`: in each aligned run of 8 customer blocks (the rows of one index of fac), every owner is named exactly 1 times. `block_counts`: every owner has some scenario with all 128 slots live.
All inputs are finite; a program needn't handle non-finite values.
Results may differ from a plain program's by a relative error of at most 0.0003.
Values may be sent and summed in bfloat16 or wider, within the bound.
A program may use at most 64 MiB of HBM per device.

v0:
```python
import jax
import jax.numpy as jnp
from jax import lax
from jax.sharding import PartitionSpec as P

TILE = 64
CBD = 8
FBD = 40


def tile_terms(tile_set, row_set, col_set, live_count, weight, block_duals):
    slot_count = tile_set.shape[0]
    periods = block_duals.shape[1] // TILE
    square_set = tile_set.reshape(slot_count, TILE, TILE)
    picked = jnp.take(block_duals, row_set, axis=0).reshape(slot_count, TILE, periods)
    products = jnp.einsum("tji,tip->tjp", square_set, picked, preferred_element_type=jnp.float32)
    position = jnp.arange(slot_count, dtype=jnp.int32)
    scaled = jnp.where(position < live_count, weight, jnp.float32(0.0))
    weighted = (products * scaled[:, None, None]).reshape(slot_count, TILE * periods)
    upper = lax.optimization_barrier(weighted.astype(jnp.bfloat16))
    lower = (weighted - upper.astype(jnp.float32)).astype(jnp.bfloat16)
    selector = (col_set[None, :] == jnp.arange(FBD, dtype=jnp.int32)[:, None]).astype(jnp.bfloat16)
    folded = jnp.dot(selector, upper, preferred_element_type=jnp.float32)
    return folded + jnp.dot(selector, lower, preferred_element_type=jnp.float32)


def local(duals, tiles, tile_rows, tile_cols, block_counts, probabilities, customer_map, costs):
    scen_local = duals.shape[0]
    periods = duals.shape[2]
    source = lax.axis_index("fac")
    local_map = lax.dynamic_slice_in_dim(customer_map, source * CBD, CBD)
    ordering = jnp.argsort(local_map * CBD + jnp.arange(CBD, dtype=jnp.int32))
    grouped = duals.reshape(scen_local, CBD, TILE * periods)
    outgoing = jnp.take(grouped, ordering, axis=1)
    arrived = lax.all_to_all(outgoing, "fac", split_axis=1, concat_axis=1, tiled=True)

    def scenario_sum(running, inputs):
        tile_set, row_set, col_set, live_count, weight, block_duals = inputs
        running = running + tile_terms(tile_set, row_set, col_set, live_count, weight, block_duals)
        return (running, None)

    initial = jnp.zeros((FBD, TILE * periods), jnp.float32)
    gradient = lax.scan(
        scenario_sum,
        initial,
        (tiles, tile_rows, tile_cols, block_counts[:, 0], probabilities, arrived),
    )[0]
    gradient_rows = gradient.reshape(FBD * TILE, periods)
    summed = lax.psum(gradient_rows, "scen")
    return costs - summed


def solution(mesh):
    in_specs = (
        P("scen", "fac", None),
        P("scen", "fac", None),
        P("scen", "fac"),
        P("scen", "fac"),
        P("scen", "fac"),
        P("scen"),
        P(),
        P("fac", None),
    )
    out_specs = P("fac", None)
    return jax.shard_map(local, mesh=mesh, in_specs=in_specs, out_specs=out_specs, check_vma=False)
```

profile of v0, /device:TPU:1, one launch (start us, length us, event | category | flops | bytes accessed | tf_op | source)
XLA Modules:
  0.0 372.0 jit_solution(14692011291748365948)
XLA Ops:
  12.1 9.1 %all-to-all-start = ((bf16[8,8,8192]{2,0,1:T(8,128)(2,1)}), bf16[8,8,8192]{2,0,1:T(8,128)(2,1)S(1)}, u32[]{:S(2)}, u32[]{:S(2)}) async-start(bf16[8,8,8192]{2,0,1:T(8,128)(2,1)} %select_bitcast_fusion), calls=%async_computation | async-start | bytes 2097152 | tf_op jit(solution)/shard_map/all_to_all | solution.py:35
  21.3 29.1 %all-to-all-done = bf16[8,8,8192]{2,0,1:T(8,128)(2,1)S(1)} async-done(((bf16[8,8,8192]{2,0,1:T(8,128)(2,1)}), bf16[8,8,8192]{2,0,1:T(8,128)(2,1)S(1)}, u32[]{:S(2)}, u32[]{:S(2)}) %all-to-all-start) | async-done | bytes 1048608 | tf_op jit(solution)/shard_map/all_to_all | solution.py:35
  51.1 197.4 %while.11 = (s32[]{:T(128)}, f32[40,8192]{1,0:T(8,128)}, s32[8,128]{1,0:T(8,128)}, bf16[8,128,4096]{2,1,0:T(8,128)(2,1)}, s32[8,128]{1,0:T(8,128)}, /*index=5*/b...) while((s32[]{:T(128)}, f32[40,8192]{1,0:T(8,128)}, ...), condition=%wide.region_2.3_spmd.clone, body=%wide.region_1.2_spmd.clone.sunk | while | flops 308228480 | bytes 65284120 | solution.py:43
  57.8 3.0 copy.30
  60.8 3.2 gather_fusion
  67.3 3.3 copy.32
  82.5 3.0 copy.30
  85.5 3.2 gather_fusion
  92.0 3.3 copy.32
  107.2 3.0 copy.30
  110.1 3.2 gather_fusion
  116.6 3.3 copy.32
  121.3 2.8 fusion.26
  131.8 3.0 copy.30
  134.8 3.2 gather_fusion
  141.3 3.3 copy.32
  156.5 3.0 copy.30
  159.5 3.2 gather_fusion
  166.0 3.3 copy.32
  170.6 2.8 fusion.26
  181.1 3.0 copy.30
  184.1 3.2 gather_fusion
  190.6 3.3 copy.32
  195.3 2.8 fusion.26
  205.8 3.0 copy.30
  208.8 3.2 gather_fusion
  215.3 3.3 copy.32
  219.9 2.8 fusion.26
  230.5 3.0 copy.30
  233.5 3.2 gather_fusion
  240.0 3.3 copy.32
  251.0 111.6 %all-reduce.2.cloned.1.call-done = f32[2560,128]{1,0:T(8,128)} async-done(((f32[2560,128]{1,0:T(8,128)}), f32[2560,128]{1,0:T(8,128)}) %all-reduce.2.cloned.1.call-update) | async-done | bytes 1310736 | tf_op jit(solution)/shard_map/psum | solution.py:49
  (202 shorter events, 120.7 us)
Async XLA Ops:
  12.1 38.9 %copy-start.5 = (s32[8,1]{0,1:T(1,128)S(1)}, s32[8,1]{0,1:T(1,128)}, u32[]{:S(2)}) copy-start(s32[8,1]{0,1:T(1,128)} %param.14) | copy-start | bytes 100
  12.1 38.9 %copy-start.6 = (f32[8]{0:T(128)S(1)}, f32[8]{0:T(128)}, u32[]{:S(2)}) copy-start(f32[8]{0:T(128)} %param.15) | copy-start | bytes 100
  12.1 38.3 %all-to-all-start = ((bf16[8,8,8192]{2,0,1:T(8,128)(2,1)}), bf16[8,8,8192]{2,0,1:T(8,128)(2,1)S(1)}, u32[]{:S(2)}, u32[]{:S(2)}) async-start(bf16[8,8,8192]{2,0,1:T(8,128)(2,1)} %select_bitcast_fusion), calls=%async_computation | async-start | bytes 2097152 | tf_op jit(solution)/shard_map/all_to_all | solution.py:35
  21.3 341.3 %all-reduce.2.cloned.1.call-start = ((), (), s32[]{:S(2)}) async-start(), calls=%async_computation.1 | async-start | bytes 2621440 | tf_op jit(solution)/shard_map/psum | solution.py:49
  51.1 6.7 %copy-start.2 = (bf16[8,8,8192]{2,1,0:T(8,128)(2,1)}, bf16[8,8,8192]{2,1,0:T(8,128)(2,1)S(1)}, u32[]{:S(2)}) copy-start(bf16[8,8,8192]{2,1,0:T(8,128)(2,1)S(1)} %get-tuple-element.183) | copy-start | bytes 3145732 | tf_op jit(solution)/shard_map/while
  70.6 1.3 copy-start
  71.9 3.8 %copy-start.3 = (bf16[8,8,8192]{2,1,0:T(8,128)(2,1)S(1)}, bf16[8,8,8192]{2,1,0:T(8,128)(2,1)}, u32[]{:S(2)}) copy-start(bf16[8,8,8192]{2,1,0:T(8,128)(2,1)} %copy-done.2) | copy-start | bytes 3145732 | tf_op jit(solution)/shard_map/while
  74.7 1.1 copy-start.1
  75.8 6.7 %copy-start.2 = (bf16[8,8,8192]{2,1,0:T(8,128)(2,1)}, bf16[8,8,8192]{2,1,0:T(8,128)(2,1)S(1)}, u32[]{:S(2)}) copy-start(bf16[8,8,8192]{2,1,0:T(8,128)(2,1)S(1)} %get-tuple-element.183) | copy-start | bytes 3145732 | tf_op jit(solution)/shard_map/while
  95.3 1.3 copy-start
  96.6 3.8 %copy-start.3 = (bf16[8,8,8192]{2,1,0:T(8,128)(2,1)S(1)}, bf16[8,8,8192]{2,1,0:T(8,128)(2,1)}, u32[]{:S(2)}) copy-start(bf16[8,8,8192]{2,1,0:T(8,128)(2,1)} %copy-done.2) | copy-start | bytes 3145732 | tf_op jit(solution)/shard_map/while
  100.4 6.7 %copy-start.2 = (bf16[8,8,8192]{2,1,0:T(8,128)(2,1)}, bf16[8,8,8192]{2,1,0:T(8,128)(2,1)S(1)}, u32[]{:S(2)}) copy-start(bf16[8,8,8192]{2,1,0:T(8,128)(2,1)S(1)} %get-tuple-element.183) | copy-start | bytes 3145732 | tf_op jit(solution)/shard_map/while
  119.9 1.3 copy-start
  121.3 3.8 %copy-start.3 = (bf16[8,8,8192]{2,1,0:T(8,128)(2,1)S(1)}, bf16[8,8,8192]{2,1,0:T(8,128)(2,1)}, u32[]{:S(2)}) copy-start(bf16[8,8,8192]{2,1,0:T(8,128)(2,1)} %copy-done.2) | copy-start | bytes 3145732 | tf_op jit(solution)/shard_map/while
  124.1 1.1 copy-start.1
  125.1 6.7 %copy-start.2 = (bf16[8,8,8192]{2,1,0:T(8,128)(2,1)}, bf16[8,8,8192]{2,1,0:T(8,128)(2,1)S(1)}, u32[]{:S(2)}) copy-start(bf16[8,8,8192]{2,1,0:T(8,128)(2,1)S(1)} %get-tuple-element.183) | copy-start | bytes 3145732 | tf_op jit(solution)/shard_map/while
  144.6 1.3 copy-start
  145.9 3.8 %copy-start.3 = (bf16[8,8,8192]{2,1,0:T(8,128)(2,1)S(1)}, bf16[8,8,8192]{2,1,0:T(8,128)(2,1)}, u32[]{:S(2)}) copy-start(bf16[8,8,8192]{2,1,0:T(8,128)(2,1)} %copy-done.2) | copy-start | bytes 3145732 | tf_op jit(solution)/shard_map/while
  149.8 6.7 %copy-start.2 = (bf16[8,8,8192]{2,1,0:T(8,128)(2,1)}, bf16[8,8,8192]{2,1,0:T(8,128)(2,1)S(1)}, u32[]{:S(2)}) copy-start(bf16[8,8,8192]{2,1,0:T(8,128)(2,1)S(1)} %get-tuple-element.183) | copy-start | bytes 3145732 | tf_op jit(solution)/shard_map/while
  169.3 1.3 copy-start
  170.6 3.8 %copy-start.3 = (bf16[8,8,8192]{2,1,0:T(8,128)(2,1)S(1)}, bf16[8,8,8192]{2,1,0:T(8,128)(2,1)}, u32[]{:S(2)}) copy-start(bf16[8,8,8192]{2,1,0:T(8,128)(2,1)} %copy-done.2) | copy-start | bytes 3145732 | tf_op jit(solution)/shard_map/while
  174.4 6.7 %copy-start.2 = (bf16[8,8,8192]{2,1,0:T(8,128)(2,1)}, bf16[8,8,8192]{2,1,0:T(8,128)(2,1)S(1)}, u32[]{:S(2)}) copy-start(bf16[8,8,8192]{2,1,0:T(8,128)(2,1)S(1)} %get-tuple-element.183) | copy-start | bytes 3145732 | tf_op jit(solution)/shard_map/while
  193.9 1.3 copy-start
  195.3 3.8 %copy-start.3 = (bf16[8,8,8192]{2,1,0:T(8,128)(2,1)S(1)}, bf16[8,8,8192]{2,1,0:T(8,128)(2,1)}, u32[]{:S(2)}) copy-start(bf16[8,8,8192]{2,1,0:T(8,128)(2,1)} %copy-done.2) | copy-start | bytes 3145732 | tf_op jit(solution)/shard_map/while
  198.0 1.1 copy-start.1
  199.1 6.7 %copy-start.2 = (bf16[8,8,8192]{2,1,0:T(8,128)(2,1)}, bf16[8,8,8192]{2,1,0:T(8,128)(2,1)S(1)}, u32[]{:S(2)}) copy-start(bf16[8,8,8192]{2,1,0:T(8,128)(2,1)S(1)} %get-tuple-element.183) | copy-start | bytes 3145732 | tf_op jit(solution)/shard_map/while
  218.6 1.3 copy-start
  219.9 3.8 %copy-start.3 = (bf16[8,8,8192]{2,1,0:T(8,128)(2,1)S(1)}, bf16[8,8,8192]{2,1,0:T(8,128)(2,1)}, u32[]{:S(2)}) copy-start(bf16[8,8,8192]{2,1,0:T(8,128)(2,1)} %copy-done.2) | copy-start | bytes 3145732 | tf_op jit(solution)/shard_map/while
  223.8 6.7 %copy-start.2 = (bf16[8,8,8192]{2,1,0:T(8,128)(2,1)}, bf16[8,8,8192]{2,1,0:T(8,128)(2,1)S(1)}, u32[]{:S(2)}) copy-start(bf16[8,8,8192]{2,1,0:T(8,128)(2,1)S(1)} %get-tuple-element.183) | copy-start | bytes 3145732 | tf_op jit(solution)/shard_map/while
  243.3 1.3 copy-start
  244.6 3.8 %copy-start.3 = (bf16[8,8,8192]{2,1,0:T(8,128)(2,1)S(1)}, bf16[8,8,8192]{2,1,0:T(8,128)(2,1)}, u32[]{:S(2)}) copy-start(bf16[8,8,8192]{2,1,0:T(8,128)(2,1)} %copy-done.2) | copy-start | bytes 3145732 | tf_op jit(solution)/shard_map/while
  248.4 114.2 %copy-start.4 = (f32[2560,128]{1,0:T(8,128)S(1)}, f32[2560,128]{1,0:T(8,128)}, u32[]{:S(2)}) copy-start(f32[2560,128]{1,0:T(8,128)} %param.17) | copy-start | bytes 3932164
  (5 other events, 5.3 us)
Sparse Core Ops, SparseCore 0:
  251.2 111.3 all-reduce.1
where the time goes:
time: 374 us; the launch traced here: 372 us
  local copies, waits for them, and re-layouts  147 us (39%)
  waiting for transfers between devices  141 us (38%)
  matrix products  31 us (8%)
  other arithmetic  29.6 us (8%)
  between operations  13.5 us (4%)
  starting transfers between devices  9.18 us (2%)
    psum x1, waiting for transfers between devices, local(): summed = lax.psum(gradient_rows, 'scen')  112 us
    while x80, local copies, waits for them, and re-layouts  59.4 us
    all_to_all x1, waiting for transfers between devices, local(): lax.all_to_all(outgoing, 'fac', split_axis=1, concat_axis=1, tiled=True)  29.1 us
    dynamic_slice x32, local copies, waits for them, and re-layouts, local(): lax.scan(scenario_sum, initial, (tiles, tile_rows, tile_cols, block_count...  26.5 us
    gather x8, local copies, waits for them, and re-layouts, tile_terms(): jnp.take(block_duals, row_set, axis=0).reshape(slot_count, TILE, periods)  25.6 us
    reshape x8, local copies, waits for them, and re-layouts, tile_terms(): square_set = tile_set.reshape(slot_count, TILE, TILE)  23.9 us
    dot_general x8, matrix products, tile_terms(): return folded + jnp.dot(selector, lower, preferred_element_type=jnp.float32)  22.2 us
    select_n x8, other arithmetic, tile_terms(): scaled = jnp.where(position < live_count, weight, jnp.float32(0.0))  9.91 us
  transfers between devices with their start and end apart: 2, of which 2 were waited for; matrix products, arithmetic and copies ran while one was open for 0% of the time, Pallas kernels for 0%

commit v1 on v0

v1 whole, which is shorter than its diff:
```python
import functools

import jax
import jax.numpy as jnp
from jax import lax
from jax.experimental import pallas as pl
from jax.experimental.pallas import tpu as pltpu
from jax.sharding import PartitionSpec as P

TILE = 64
FBD = 40
SLOTS = 128
LANES = 128
PAIRS = TILE // 2
WIDE = 16
HALF = PAIRS * FBD
MESH = pl.DeviceIdType.MESH


def exchange_kernel(
    ny,
    nx,
    nz,
    scen,
    duals_hbm,
    tiles_hbm,
    rows_ref,
    cols_ref,
    counts_ref,
    prob_ref,
    map_ref,
    out_hbm,
    duals_v,
    tiles_v,
    stage,
    land,
    selector,
    high,
    low,
    weights,
    acc,
    core_in,
    x_in,
    y_in,
    x_sum,
    y_sum,
    x_in2,
    y_in2,
    full,
    duals_sem,
    tiles_sem,
    z_send,
    z_recv,
    c_send,
    c_recv,
    r_send,
    r_recv,
    q_send,
    q_recv,
    g_send,
    g_recv,
    h_send,
    h_recv,
    f_send,
    f_recv,
    out_sem,
):
    sc = lax.axis_index("scen")
    me = lax.axis_index("fac")
    core = lax.rem(sc, 2)
    xx = lax.rem(lax.div(sc, 2), nx)
    yy = lax.div(sc, 2 * nx)

    def at(y, x, c):
        return (lax.rem(y, ny) * nx + lax.rem(x, nx)) * 2 + c

    duals_copy = pltpu.make_async_copy(duals_hbm, duals_v, duals_sem)
    duals_copy.start()

    barrier = pltpu.get_barrier_semaphore()
    peers = 0
    for d in range(1, nz):
        pl.semaphore_signal(barrier, inc=1, device_id=(sc, lax.rem(me + d, nz)), device_id_type=MESH)
        peers += 1
    for d in range(1, nx):
        pl.semaphore_signal(barrier, inc=1, device_id=(at(yy, xx + d, core), me), device_id_type=MESH)
        peers += 1
    for d in range(1, ny):
        pl.semaphore_signal(barrier, inc=1, device_id=(at(yy + d, xx, core), me), device_id_type=MESH)
        peers += 1
    pl.semaphore_signal(barrier, inc=1, device_id=(at(yy, xx, 1 - core), me), device_id_type=MESH)
    peers += 1

    def tiles_copy(s):
        return pltpu.make_async_copy(tiles_hbm.at[s], tiles_v.at[s], tiles_sem.at[s])

    @pl.loop(0, scen)
    def _(s):
        tiles_copy(s).start()

    owners = [map_ref[me * nz + k] for k in range(nz)]
    keep = [[jnp.where(owner == o, 1.0, 0.0) for owner in owners] for o in range(nz)]

    weights[...] = jnp.zeros_like(weights)
    acc[...] = jnp.zeros_like(acc)
    duals_copy.wait()

    @pl.loop(0, scen)
    def _(s):
        blocks = [duals_v[s, k * TILE : (k + 1) * TILE, :].astype(jnp.float32) for k in range(nz)]
        for o in range(nz):
            block = blocks[0] * keep[o][0]
            for k in range(1, nz):
                block = block + blocks[k] * keep[o][k]
            stage[s, o] = block.astype(jnp.bfloat16)

    pl.semaphore_wait(barrier, peers)

    def z_copy(s, d):
        to = lax.rem(me + d, nz)
        return pltpu.make_async_remote_copy(
            src_ref=stage.at[s, to],
            dst_ref=land.at[s, me],
            send_sem=z_send.at[s, d],
            recv_sem=z_recv.at[s, d],
            device_id=(sc, to),
            device_id_type=MESH,
        )

    def z_arrival(s, d):
        source = lax.rem(me + nz - d, nz)
        return pltpu.make_async_remote_copy(
            src_ref=stage.at[s, source],
            dst_ref=land.at[s, source],
            send_sem=z_send.at[s, d],
            recv_sem=z_recv.at[s, d],
            device_id=(sc, source),
            device_id_type=MESH,
        )

    order = sorted(range(1, nz), key=lambda d: -min(d, nz - d))

    @pl.loop(0, scen)
    def _(s):
        for d in order:
            z_copy(s, d).start()
        land[s, me] = stage[s, me]

    position = lax.broadcasted_iota(jnp.int32, rows_ref.shape, 1)
    cells = jnp.where(position < counts_ref[...], rows_ref[...] * FBD + cols_ref[...], -1)
    cell_ids = lax.broadcasted_iota(jnp.int32, (nz * FBD, SLOTS), 0)
    row_ids = lax.broadcasted_iota(jnp.int32, rows_ref.shape, 0)

    @pl.loop(0, scen)
    def _(s):
        mine = jnp.sum(jnp.where(row_ids == s, cells, 0), axis=0, keepdims=True)
        selector[...] = jnp.where(cell_ids == mine, 1.0, 0.0).astype(jnp.bfloat16)
        tiles_copy(s).wait()

        for n in range(WIDE):
            block = tiles_v[s, :, n * 256 : (n + 1) * 256]
            dense = jnp.dot(selector[...], block, preferred_element_type=jnp.float32)
            for r in range(nz):
                part = dense[r * FBD : (r + 1) * FBD]
                both = jnp.concatenate([part[:, :LANES], part[:, LANES:]], axis=0)
                upper = both.astype(jnp.bfloat16)
                lower = (both - upper.astype(jnp.float32)).astype(jnp.bfloat16)
                high[n * 80 : (n + 1) * 80, r * LANES : (r + 1) * LANES] = upper
                low[n * 80 : (n + 1) * 80, r * LANES : (r + 1) * LANES] = lower

        for d in range(1, nz):
            z_arrival(s, d).wait_recv()
        for r in range(nz):
            block = land[s, r]
            weights[r * LANES : r * LANES + TILE, :LANES] = block
            weights[r * LANES + TILE : (r + 1) * LANES, LANES:] = block

        scale = prob_ref[s]
        for n in range(4):
            rows = slice(n * 320, (n + 1) * 320)
            value = jnp.dot(high[rows], weights[...], preferred_element_type=jnp.float32)
            value = value + jnp.dot(low[rows], weights[...], preferred_element_type=jnp.float32)
            value = value * scale
            acc[n * 320 : (n + 1) * 320, :] += value[:, :LANES]
            acc[HALF + n * 320 : HALF + (n + 1) * 320, :] += value[:, LANES:]

    @pl.loop(0, scen)
    def _(s):
        for d in range(1, nz):
            z_copy(s, d).wait_send()

    part = HALF // 2
    mine = core * HALF
    other = (1 - core) * HALF
    sibling = (at(yy, xx, 1 - core), me)

    def core_copy(k):
        return pltpu.make_async_remote_copy(
            src_ref=acc.at[pl.ds(other + k * part, part)],
            dst_ref=core_in.at[pl.ds(k * part, part)],
            send_sem=c_send.at[k],
            recv_sem=c_recv.at[k],
            device_id=sibling,
            device_id_type=MESH,
        )

    for k in range(2):
        core_copy(k).start()

    first = (nx, ny)
    second = (ny, nx)
    spot = (xx, yy)
    spot2 = (yy, xx)
    inbox = (x_in, y_in)
    inbox2 = (x_in2, y_in2)
    sums = (x_sum, y_sum)

    def peer(k, d, n):
        along_x = (k == 0) == (n == 0)
        return (at(yy, xx + d, core) if along_x else at(yy + d, xx, core), me)

    def size1(k):
        return part // first[k]

    def size2(k):
        return size1(k) // second[k]

    def r_copy(k, d):
        to = lax.rem(spot[k] + d, first[k])
        return pltpu.make_async_remote_copy(
            src_ref=acc.at[pl.ds(mine + k * part + to * size1(k), size1(k))],
            dst_ref=inbox[k].at[d - 1],
            send_sem=r_send.at[k, d],
            recv_sem=r_recv.at[k, d],
            device_id=peer(k, d, 0),
            device_id_type=MESH,
        )

    def q_copy(k, d):
        to = lax.rem(spot2[k] + d, second[k])
        return pltpu.make_async_remote_copy(
            src_ref=sums[k].at[pl.ds(to * size2(k), size2(k))],
            dst_ref=inbox2[k].at[d - 1],
            send_sem=q_send.at[k, d],
            recv_sem=q_recv.at[k, d],
            device_id=peer(k, d, 1),
            device_id_type=MESH,
        )

    def big(k, x):
        return mine + k * part + x * size1(k)

    def small(k, y):
        return big(k, spot[k]) + y * size2(k)

    def g_copy(k, d, y):
        rows = full.at[pl.ds(small(k, y), size2(k))]
        return pltpu.make_async_remote_copy(
            src_ref=rows,
            dst_ref=rows,
            send_sem=g_send.at[k, d],
            recv_sem=g_recv.at[k, d],
            device_id=peer(k, d, 1),
            device_id_type=MESH,
        )

    def h_copy(k, d, x):
        rows = full.at[pl.ds(big(k, x), size1(k))]
        return pltpu.make_async_remote_copy(
            src_ref=rows,
            dst_ref=rows,
            send_sem=h_send.at[k, d],
            recv_sem=h_recv.at[k, d],
            device_id=peer(k, d, 0),
            device_id_type=MESH,
        )

    def f_copy(k, d, base):
        x = lax.rem(spot[k] + first[k] - d, first[k])
        rows = full.at[pl.ds(base + k * part + x * size1(k), size1(k))]
        return pltpu.make_async_remote_copy(
            src_ref=rows,
            dst_ref=rows,
            send_sem=f_send.at[k, d],
            recv_sem=f_recv.at[k, d],
            device_id=sibling,
            device_id_type=MESH,
        )

    for k in range(2):
        core_copy(k).wait_recv()
        here = pl.ds(mine + k * part, part)
        acc[here, :] += core_in[k * part : (k + 1) * part, :]
        for d in range(1, first[k]):
            r_copy(k, d).start()
    for k in range(2):
        total = acc[pl.ds(big(k, spot[k]), size1(k)), :]
        for d in range(1, first[k]):
            r_copy(k, d).wait_recv()
            total = total + inbox[k][d - 1]
        sums[k][...] = total
        for d in range(1, second[k]):
            q_copy(k, d).start()
    for k in range(2):
        total = sums[k][pl.ds(spot2[k] * size2(k), size2(k)), :]
        for d in range(1, second[k]):
            q_copy(k, d).wait_recv()
            total = total + inbox2[k][d - 1]
        full[pl.ds(small(k, spot2[k]), size2(k)), :] = total
        for d in range(1, second[k]):
            g_copy(k, d, spot2[k]).start()
    for k in range(2):
        for d in range(1, second[k]):
            g_copy(k, d, lax.rem(spot2[k] + second[k] - d, second[k])).wait_recv()
        for d in range(1, first[k]):
            h_copy(k, d, spot[k]).start()
        f_copy(k, 0, mine).start()
    for d in range(1, max(first)):
        for k in range(2):
            if d < first[k]:
                h_copy(k, d, lax.rem(spot[k] + first[k] - d, first[k])).wait_recv()
                f_copy(k, d, mine).start()
    for k in range(2):
        for d in range(first[k]):
            f_copy(k, d, other).wait_recv()
    out_copy = pltpu.make_async_copy(full, out_hbm, out_sem)
    out_copy.start()
    for k in range(2):
        core_copy(k).wait_send()
        for d in range(1, first[k]):
            r_copy(k, d).wait_send()
            h_copy(k, d, spot[k]).wait_send()
        for d in range(1, second[k]):
            q_copy(k, d).wait_send()
            g_copy(k, d, spot2[k]).wait_send()
        for d in range(first[k]):
            f_copy(k, d, mine).wait_send()
    out_copy.wait()


def finish_kernel(costs_ref, gradient_ref, out_ref):
    for j in range(TILE):
        at = (j % 2) * HALF + (j // 2) * FBD
        rows = pl.ds(j, FBD, stride=TILE)
        out_ref[rows, :] = costs_ref[rows, :] - gradient_ref[at : at + FBD, :]


def local(ny, nx, nz, duals, tiles, tile_rows, tile_cols, block_counts, probabilities, customer_map, costs):
    scen = duals.shape[0]
    bf16, f32 = jnp.bfloat16, jnp.float32
    part = HALF // 2
    vmem = pl.BlockSpec(memory_space=pltpu.VMEM)
    smem = pl.BlockSpec(memory_space=pltpu.SMEM)
    far = pl.BlockSpec(memory_space=pl.ANY)
    dma = pltpu.SemaphoreType.DMA
    most = max(nx, ny)
    gradient = pl.pallas_call(
        functools.partial(exchange_kernel, ny, nx, nz, scen),
        out_shape=jax.ShapeDtypeStruct((2 * HALF, LANES), f32),
        in_specs=[far, far, vmem, vmem, vmem, smem, smem],
        out_specs=far,
        scratch_shapes=[
            pltpu.VMEM(duals.shape, bf16),
            pltpu.VMEM(tiles.shape, bf16),
            pltpu.VMEM((scen, nz, TILE, LANES), bf16),
            pltpu.VMEM((scen, nz, TILE, LANES), bf16),
            pltpu.VMEM((nz * FBD, SLOTS), bf16),
            pltpu.VMEM((HALF, nz * LANES), bf16),
            pltpu.VMEM((HALF, nz * LANES), bf16),
            pltpu.VMEM((nz * LANES, 2 * LANES), bf16),
            pltpu.VMEM((2 * HALF, LANES), f32),
            pltpu.VMEM((HALF, LANES), f32),
            pltpu.VMEM((nx - 1, part // nx, LANES), f32),
            pltpu.VMEM((ny - 1, part // ny, LANES), f32),
            pltpu.VMEM((part // nx, LANES), f32),
            pltpu.VMEM((part // ny, LANES), f32),
            pltpu.VMEM((ny - 1, part // nx // ny, LANES), f32),
            pltpu.VMEM((nx - 1, part // nx // ny, LANES), f32),
            pltpu.VMEM((2 * HALF, LANES), f32),
            dma,
            dma((scen,)),
            dma((scen, nz)),
            dma((scen, nz)),
            dma((2,)),
            dma((2,)),
            dma((2, most)),
            dma((2, most)),
            dma((2, most)),
            dma((2, most)),
            dma((2, most)),
            dma((2, most)),
            dma((2, most)),
            dma((2, most)),
            dma((2, most)),
            dma((2, most)),
            dma,
        ],
        compiler_params=pltpu.CompilerParams(
            collective_id=0, has_side_effects=True, vmem_limit_bytes=48 * 2**20
        ),
        name="exchange",
    )(duals, tiles, tile_rows, tile_cols, block_counts, probabilities, customer_map)
    return pl.pallas_call(
        finish_kernel,
        out_shape=jax.ShapeDtypeStruct(costs.shape, f32),
        in_specs=[vmem, vmem],
        out_specs=vmem,
        compiler_params=pltpu.CompilerParams(vmem_limit_bytes=32 * 2**20),
        name="finish",
    )(costs, gradient)


def solution(mesh):
    nz = mesh.shape["fac"]
    chips = mesh.shape["scen"] // 2
    side = 1
    while side * side < chips:
        side += 1
    in_specs = (
        P("scen", "fac", None),
        P("scen", "fac", None),
        P("scen", "fac"),
        P("scen", "fac"),
        P("scen", "fac"),
        P("scen"),
        P(),
        P("fac", None),
    )
    out_specs = P("fac", None)
    return jax.shard_map(
        functools.partial(local, side, side, nz),
        mesh=mesh,
        in_specs=in_specs,
        out_specs=out_specs,
        check_vma=False,
    )
```

time: 374 us -> 71 us (0.19)
  local copies, waits for them, and re-layouts: 147 us -> 4.64 us
  waiting for transfers between devices: 141 us -> 0 us
  Pallas kernels: 0 us -> 66.1 us
  matrix products: 31 us -> 0 us
  other arithmetic: 29.6 us -> 0 us
  between operations: 13.5 us -> 0.02 us
  starting transfers between devices: 9.18 us -> 0 us
    psum x1 -> x0, waiting for transfers between devices: 112 us -> none  [local(): summed = lax.psum(gradient_rows, 'scen')]
    pallas_call x0 -> x2, Pallas kernels: none -> 66.1 us  [the longest x1 63.6 us: local(): pl.pallas_call(functools.partial(exchange_kernel, ny, nx, nz, scen), out_...]
    while x80 -> x0, local copies, waits for them, and re-layouts: 59.4 us -> none
    dot_general x24 -> x0, matrix products: 31 us -> none  [the longest x8 22.2 us: tile_terms(): return folded + jnp.dot(selector, lower, preferred_element_type=jnp.float32)]
    all_to_all x1 -> x0, waiting for transfers between devices: 29.1 us -> none  [local(): lax.all_to_all(outgoing, 'fac', split_axis=1, concat_axis=1, tiled=True)]
    reshape x11 -> x0, local copies, waits for them, and re-layouts: 28.6 us -> none  [the longest x8 23.9 us: tile_terms(): square_set = tile_set.reshape(slot_count, TILE, TILE)]
    dynamic_slice x32 -> x0, local copies, waits for them, and re-layouts: 26.5 us -> none  [local(): lax.scan(scenario_sum, initial, (tiles, tile_rows, tile_cols, block_count...]
    gather x9 -> x0, local copies, waits for them, and re-layouts: 26.2 us -> none  [the longest x8 25.6 us: tile_terms(): jnp.take(block_duals, row_set, axis=0).reshape(slot_count, TILE, periods)]
  transfers between devices with their start and end apart: 2 -> 0, of which waited for: 2 -> 0; matrix products, arithmetic and copies ran while one was open for 0% -> 0% of each run, Pallas kernels for 0% -> 0%
where the time goes in v1:
time: 71 us; the launch traced here: 70.8 us
  Pallas kernels  66.1 us (93%)
  local copies, waits for them, and re-layouts  4.64 us (7%)
    pallas_call x1, Pallas kernels, local(): pl.pallas_call(functools.partial(exchange_kernel, ny, nx, nz, scen), out_...  63.6 us
    unnamed x13, local copies, waits for them, and re-layouts  4.64 us
    pallas_call x1, Pallas kernels, local(): pl.pallas_call(finish_kernel, out_shape=jax.ShapeDtypeStruct(costs.shape,...  2.53 us

profile of v1, /device:TPU:1, one launch (start us, length us, event | category | flops | bytes accessed | tf_op | source)
XLA Modules:
  0.0 70.8 jit_solution(7420523088764660689)
XLA Ops:
  0.0 0.7 %copy.9.counts_ref = s32[8,1]{1,0:T(8,128)S(1)} copy(s32[8,1]{0,1:T(1,128)} %param.12) | data formatting | bytes 64 | tf_op args[4]
  0.7 0.0 copy-start.1
  0.7 1.2 %copy-done.1 = bf16[8,512,128]{2,1,0:T(8,128)(2,1)S(1)} copy-done((bf16[8,512,128]{2,1,0:T(8,128)(2,1)S(1)}, bf16[8,512,128]{2,1,0:T(8,128)(2,1)}, u32[]{:S(2)}) %copy-start.1) | copy-done | bytes 1048600
  2.0 0.0 copy-start.2
  2.0 0.7 copy-done.2
  2.6 0.0 copy-start.3
  2.6 0.7 copy-done.3
  3.3 0.0 copy-start.4
  3.3 0.7 copy-done.4
  4.0 0.0 copy-start.5
  4.0 0.7 copy-done.5
  4.6 0.0 copy-start
  4.6 63.6 %exchange.1.gradient_ref = f32[2560,128]{1,0:T(8,128)S(1)} custom-call(bf16[8,512,128]{2,1,0:T(8,128)(2,1)S(1)} %copy-done.1, bf16[8,128,4096]{2,1,0:T(8,128)(2,1)} %tiles_hbm.1, s32[8,128]{1,0:T(8,128)S(1)} %copy-done.2, s32[8,128]{1,0:T(8,128)S(1)} %copy-done.3, s32[8,1]{1,0:T(8,128)S(1)} %copy.9.counts_ref, f32[8]{0:T(128)S(1)} %copy-done.4, s32[64]{0:T(128)S(1)} %copy-done.5), custom_call_target="tpu_custom_call" | custom-call | tf_op jit(solution)/shard_map/exchange/pallas_call | solution.py:357
  68.2 0.0 copy-done
  68.2 2.5 %finish.1 = f32[2560,128]{1,0:T(8,128)} custom-call(f32[2560,128]{1,0:T(8,128)S(1)} %copy-done, f32[2560,128]{1,0:T(8,128)S(1)} %exchange.1.gradient_ref), custom_call_target="tpu_custom_call" | custom-call | tf_op jit(solution)/shard_map/finish/pallas_call | solution.py:403
Async XLA Ops:
  0.7 1.2 %copy-start.1 = (bf16[8,512,128]{2,1,0:T(8,128)(2,1)S(1)}, bf16[8,512,128]{2,1,0:T(8,128)(2,1)}, u32[]{:S(2)}) copy-start(bf16[8,512,128]{2,1,0:T(8,128)(2,1)} %duals_hbm.1) | copy-start | bytes 3145732
  2.0 0.7 copy-start.2
  2.6 0.7 copy-start.3
  3.3 0.7 copy-start.4
  4.0 0.7 copy-start.5
  4.6 63.6 %copy-start = (f32[2560,128]{1,0:T(8,128)S(1)}, f32[2560,128]{1,0:T(8,128)}, u32[]{:S(2)}) copy-start(f32[2560,128]{1,0:T(8,128)} %costs_ref.1) | copy-start | bytes 3932164

commit v2 on v0

v2 whole, which is shorter than its diff:
```python
import functools

import jax
import jax.numpy as jnp
from jax import lax
from jax.experimental import pallas as pl
from jax.experimental.pallas import tpu as pltpu
from jax.sharding import PartitionSpec as P

TILE = 64
FBD = 40
SLOTS = 128
LANES = 128
PAIRS = TILE // 2
WIDE = 16
DEEP = 5
CHUNKS = ((0, 40),)
MESH = pl.DeviceIdType.MESH


def exchange_kernel(
    ny,
    nx,
    nz,
    scen,
    duals_hbm,
    tiles_hbm,
    rows_hbm,
    cols_hbm,
    counts_hbm,
    prob_hbm,
    map_hbm,
    out,
    rows_ref,
    cols_ref,
    counts_ref,
    prob_ref,
    map_ref,
    duals_v,
    tiles_v,
    stage,
    land,
    selector,
    high,
    low,
    weights,
    acc,
    core_in,
    x_in,
    y_in,
    x_sum,
    y_sum,
    x_in2,
    y_in2,
    x_last,
    y_last,
    small_sem,
    duals_sem,
    tiles_sem,
    z_send,
    z_recv,
    c_send,
    c_recv,
    r_send,
    r_recv,
    q_send,
    q_recv,
    g_send,
    g_recv,
    h_send,
    h_recv,
    f_send,
    f_recv,
    own_sem,
):
    sc = lax.axis_index("scen")
    me = lax.axis_index("fac")
    core = lax.rem(sc, 2)
    xx = lax.rem(lax.div(sc, 2), nx)
    yy = lax.div(sc, 2 * nx)

    def at(y, x, c):
        return (lax.rem(y, ny) * nx + lax.rem(x, nx)) * 2 + c

    sibling = (at(yy, xx, 1 - core), me)

    barrier = pltpu.get_barrier_semaphore()
    peers = [(sc, lax.rem(me + d, nz)) for d in range(1, nz)]
    peers += [(at(yy, xx + d, core), me) for d in range(1, nx)]
    peers += [(at(yy + d, xx, core), me) for d in range(1, ny)]
    peers.append(sibling)
    for one in peers:
        pl.semaphore_signal(barrier, inc=1, device_id=one, device_id_type=MESH)

    duals_copy = pltpu.make_async_copy(duals_hbm, duals_v, duals_sem)
    pairs = ((map_hbm, map_ref), (rows_hbm, rows_ref), (cols_hbm, cols_ref), (counts_hbm, counts_ref), (prob_hbm, prob_ref))
    smalls = [pltpu.make_async_copy(src, dst, small_sem.at[n]) for n, (src, dst) in enumerate(pairs)]
    smalls[0].start()
    duals_copy.start()
    for one in smalls[1:]:
        one.start()

    def tiles_copy(s):
        return pltpu.make_async_copy(tiles_hbm.at[s], tiles_v.at[s], tiles_sem.at[s])

    @pl.loop(0, scen)
    def _(s):
        tiles_copy(s).start()

    weights[...] = jnp.zeros_like(weights)
    acc[...] = jnp.zeros_like(acc)
    for one in smalls:
        one.wait()

    owners = [map_ref[me * nz + k] for k in range(nz)]
    keep = [[jnp.where(owner == o, 1.0, 0.0) for owner in owners] for o in range(nz)]
    duals_copy.wait()

    @pl.loop(0, scen)
    def _(s):
        blocks = [duals_v[s, k * TILE : (k + 1) * TILE, :].astype(jnp.float32) for k in range(nz)]
        for o in range(nz):
            block = blocks[0] * keep[o][0]
            for k in range(1, nz):
                block = block + blocks[k] * keep[o][k]
            stage[s, o] = block.astype(jnp.bfloat16)

    def densify(s):
        slot = lax.rem(s, DEEP)
        position = lax.broadcasted_iota(jnp.int32, (1, SLOTS), 1)
        cells = rows_ref[pl.ds(s, 1), :] * FBD + cols_ref[pl.ds(s, 1), :]
        cells = jnp.where(position < counts_ref[s], cells, -1)
        cell_ids = lax.broadcasted_iota(jnp.int32, (nz * FBD, SLOTS), 0)
        selector[...] = jnp.where(cell_ids == cells, 1.0, 0.0).astype(jnp.bfloat16)
        tiles_copy(s).wait()
        for n in range(WIDE):
            block = tiles_v[s, :, n * 256 : (n + 1) * 256]
            dense = jnp.dot(selector[...], block, preferred_element_type=jnp.float32)
            for r in range(nz):
                part = dense[r * FBD : (r + 1) * FBD]
                both = jnp.concatenate([part[:, :LANES], part[:, LANES:]], axis=0)
                upper = both.astype(jnp.bfloat16)
                lower = (both - upper.astype(jnp.float32)).astype(jnp.bfloat16)
                high[slot, n * 80 : (n + 1) * 80, r * LANES : (r + 1) * LANES] = upper
                low[slot, n * 80 : (n + 1) * 80, r * LANES : (r + 1) * LANES] = lower

    densify(0)
    pl.semaphore_wait(barrier, len(peers))

    def z_copy(s, d):
        to = lax.rem(me + d, nz)
        return pltpu.make_async_remote_copy(
            src_ref=stage.at[s, to],
            dst_ref=land.at[s, me],
            send_sem=z_send.at[s, d],
            recv_sem=z_recv.at[s, d],
            device_id=(sc, to),
            device_id_type=MESH,
        )

    def z_arrival(s, d):
        source = lax.rem(me + nz - d, nz)
        return pltpu.make_async_remote_copy(
            src_ref=stage.at[s, source],
            dst_ref=land.at[s, source],
            send_sem=z_send.at[s, d],
            recv_sem=z_recv.at[s, d],
            device_id=(sc, source),
            device_id_type=MESH,
        )

    order = sorted(range(1, nz), key=lambda d: -min(d, nz - d))

    @pl.loop(0, scen)
    def _(s):
        for d in order:
            z_copy(s, d).start()
        land[s, me] = stage[s, me]

    @pl.loop(1, min(DEEP, scen))
    def _(s):
        densify(s)

    first = (nx, ny)
    second = (ny, nx)
    spot = (xx, yy)
    spot2 = (yy, xx)
    inbox = (x_in, y_in)
    inbox2 = (x_in2, y_in2)
    sums = (x_sum, y_sum)
    last = (x_last, y_last)
    part = PAIRS // 2
    size1 = [part // n for n in first]
    size2 = [part // (ny * nx)] * 2
    mine = core * PAIRS
    other = (1 - core) * PAIRS

    def columns(h):
        return pl.ds(CHUNKS[h][0], CHUNKS[h][1])

    def core_copy(k, h):
        return pltpu.make_async_remote_copy(
            src_ref=acc.at[pl.ds(other + k * part, part), columns(h)],
            dst_ref=core_in.at[pl.ds(k * part, part), columns(h)],
            send_sem=c_send.at[k, h],
            recv_sem=c_recv.at[k, h],
            device_id=sibling,
            device_id_type=MESH,
        )

    @pl.loop(0, scen)
    def _(s):
        slot = lax.rem(s, DEEP)
        for d in range(1, nz):
            z_arrival(s, d).wait_recv()
        for r in range(nz):
            block = land[s, r]
            weights[r * LANES : r * LANES + TILE, :LANES] = block
            weights[r * LANES + TILE : (r + 1) * LANES, LANES:] = block

        scale = prob_ref[s]
        for n in range(4):
            rows = slice(n * 320, (n + 1) * 320)
            value = jnp.dot(high[slot, rows], weights[...], preferred_element_type=jnp.float32)
            value = value + jnp.dot(low[slot, rows], weights[...], preferred_element_type=jnp.float32)
            value = value * scale
            acc[n * 8 : (n + 1) * 8] += value[:, :LANES].reshape(8, FBD, LANES)
            acc[PAIRS + n * 8 : PAIRS + (n + 1) * 8] += value[:, LANES:].reshape(8, FBD, LANES)
            if n % 2:

                @pl.when(s == scen - 1)
                def _():
                    for h in range(len(CHUNKS)):
                        core_copy(n // 2, h).start()

        @pl.when(s < scen - DEEP)
        def _():
            densify(s + DEEP)

    def peer(k, d, n):
        along_x = (k == 0) == (n == 0)
        return (at(yy, xx + d, core) if along_x else at(yy + d, xx, core), me)

    def big(k, x):
        return mine + k * part + x * size1[k]

    def small(k, y):
        return big(k, spot[k]) + y * size2[k]

    def r_copy(k, h, d):
        to = lax.rem(spot[k] + d, first[k])
        return pltpu.make_async_remote_copy(
            src_ref=acc.at[pl.ds(big(k, to), size1[k]), columns(h)],
            dst_ref=inbox[k].at[d - 1, :, columns(h)],
            send_sem=r_send.at[k, h, d],
            recv_sem=r_recv.at[k, h, d],
            device_id=peer(k, d, 0),
            device_id_type=MESH,
        )

    def q_copy(k, h, d):
        to = lax.rem(spot2[k] + d, second[k])
        return pltpu.make_async_remote_copy(
            src_ref=sums[k].at[pl.ds(to * size2[k], size2[k]), columns(h)],
            dst_ref=inbox2[k].at[d - 1, :, columns(h)],
            send_sem=q_send.at[k, h, d],
            recv_sem=q_recv.at[k, h, d],
            device_id=peer(k, d, 1),
            device_id_type=MESH,
        )

    def g_copy(k, h, d, y):
        return pltpu.make_async_remote_copy(
            src_ref=last[k].at[:, columns(h)],
            dst_ref=out.at[pl.ds(small(k, y), size2[k]), columns(h)],
            send_sem=g_send.at[k, h, d],
            recv_sem=g_recv.at[k, h, d],
            device_id=peer(k, d, 1),
            device_id_type=MESH,
        )

    def own_copy(k, h):
        return pltpu.make_async_copy(
            last[k].at[:, columns(h)],
            out.at[pl.ds(small(k, spot2[k]), size2[k]), columns(h)],
            own_sem.at[k, h],
        )

    def h_copy(k, h, d, x):
        block = out.at[pl.ds(big(k, x), size1[k]), columns(h)]
        return pltpu.make_async_remote_copy(
            src_ref=block,
            dst_ref=block,
            send_sem=h_send.at[k, h, d],
            recv_sem=h_recv.at[k, h, d],
            device_id=peer(k, d, 0),
            device_id_type=MESH,
        )

    def f_copy(k, h, d, base):
        x = lax.rem(spot[k] + first[k] - d, first[k])
        block = out.at[pl.ds(base + k * part + x * size1[k], size1[k]), columns(h)]
        return pltpu.make_async_remote_copy(
            src_ref=block,
            dst_ref=block,
            send_sem=f_send.at[k, h, d],
            recv_sem=f_recv.at[k, h, d],
            device_id=sibling,
            device_id_type=MESH,
        )

    pieces = [(k, h) for h in range(len(CHUNKS)) for k in range(2)]
    for k, h in pieces:
        core_copy(k, h).wait_recv()
        here = pl.ds(mine + k * part, part)
        acc[here, columns(h)] += core_in[k * part : (k + 1) * part, columns(h)]
        for d in range(1, first[k]):
            r_copy(k, h, d).start()
    for k, h in pieces:
        total = acc[pl.ds(big(k, spot[k]), size1[k]), columns(h)]
        for d in range(1, first[k]):
            r_copy(k, h, d).wait_recv()
            total = total + inbox[k][d - 1, :, columns(h)]
        sums[k][:, columns(h)] = total
        for d in range(1, second[k]):
            q_copy(k, h, d).start()
    for k, h in pieces:
        total = sums[k][pl.ds(spot2[k] * size2[k], size2[k]), columns(h)]
        for d in range(1, second[k]):
            q_copy(k, h, d).wait_recv()
            total = total + inbox2[k][d - 1, :, columns(h)]
        last[k][:, columns(h)] = total
        for d in range(1, second[k]):
            g_copy(k, h, d, spot2[k]).start()
        own_copy(k, h).start()
    for k, h in pieces:
        own_copy(k, h).wait()
        for d in range(1, second[k]):
            g_copy(k, h, d, lax.rem(spot2[k] + second[k] - d, second[k])).wait_recv()
        for d in range(1, first[k]):
            h_copy(k, h, d, spot[k]).start()
        f_copy(k, h, 0, mine).start()
    for k, h in pieces:
        for d in range(1, first[k]):
            h_copy(k, h, d, lax.rem(spot[k] + first[k] - d, first[k])).wait_recv()
            f_copy(k, h, d, mine).start()

    @pl.loop(0, scen)
    def _(s):
        for d in range(1, nz):
            z_copy(s, d).wait_send()

    for k, h in pieces:
        core_copy(k, h).wait_send()
        for d in range(1, first[k]):
            r_copy(k, h, d).wait_send()
            h_copy(k, h, d, spot[k]).wait_send()
        for d in range(1, second[k]):
            q_copy(k, h, d).wait_send()
            g_copy(k, h, d, spot2[k]).wait_send()
        for d in range(first[k]):
            f_copy(k, h, d, mine).wait_send()
    for k, h in pieces:
        for d in range(first[k]):
            f_copy(k, h, d, other).wait_recv()


def finish_kernel(costs_ref, gradient_ref, out_hbm, out_v, sem):
    copies = []
    for q in range(FBD // 8):
        for j in range(TILE):
            rows = pl.ds(q * 8 * TILE + j, 8, stride=TILE)
            value = gradient_ref[(j % 2) * PAIRS + j // 2, q * 8 : (q + 1) * 8]
            out_v[rows, :] = costs_ref[rows, :] - value
        rows = pl.ds(q * 8 * TILE, 8 * TILE)
        copies.append(pltpu.make_async_copy(out_v.at[rows], out_hbm.at[rows], sem.at[q]))
        copies[-1].start()
    for one in copies:
        one.wait()


def local(ny, nx, nz, duals, tiles, tile_rows, tile_cols, block_counts, probabilities, customer_map, costs):
    scen = duals.shape[0]
    bf16, f32 = jnp.bfloat16, jnp.float32
    part = PAIRS // 2
    vmem = pl.BlockSpec(memory_space=pltpu.VMEM)
    far = pl.BlockSpec(memory_space=pl.ANY)
    hbm = pl.BlockSpec(memory_space=pltpu.HBM)
    dma = pltpu.SemaphoreType.DMA
    sems = dma((2, len(CHUNKS), max(nx, ny)))
    deep = min(DEEP, scen)
    gradient = pl.pallas_call(
        functools.partial(exchange_kernel, ny, nx, nz, scen),
        out_shape=jax.ShapeDtypeStruct((TILE, FBD, LANES), f32),
        in_specs=[hbm] * 7,
        out_specs=far,
        scratch_shapes=[
            pltpu.VMEM(tile_rows.shape, jnp.int32),
            pltpu.VMEM(tile_cols.shape, jnp.int32),
            pltpu.SMEM((scen,), jnp.int32),
            pltpu.SMEM((scen,), f32),
            pltpu.SMEM(customer_map.shape, jnp.int32),
            pltpu.VMEM(duals.shape, bf16),
            pltpu.VMEM(tiles.shape, bf16),
            pltpu.VMEM((scen, nz, TILE, LANES), bf16),
            pltpu.VMEM((scen, nz, TILE, LANES), bf16),
            pltpu.VMEM((nz * FBD, SLOTS), bf16),
            pltpu.VMEM((deep, PAIRS * FBD, nz * LANES), bf16),
            pltpu.VMEM((deep, PAIRS * FBD, nz * LANES), bf16),
            pltpu.VMEM((nz * LANES, 2 * LANES), bf16),
            pltpu.VMEM((TILE, FBD, LANES), f32),
            pltpu.VMEM((PAIRS, FBD, LANES), f32),
            pltpu.VMEM((nx - 1, part // nx, FBD, LANES), f32),
            pltpu.VMEM((ny - 1, part // ny, FBD, LANES), f32),
            pltpu.VMEM((part // nx, FBD, LANES), f32),
            pltpu.VMEM((part // ny, FBD, LANES), f32),
            pltpu.VMEM((ny - 1, part // nx // ny, FBD, LANES), f32),
            pltpu.VMEM((nx - 1, part // nx // ny, FBD, LANES), f32),
            pltpu.VMEM((part // nx // ny, FBD, LANES), f32),
            pltpu.VMEM((part // nx // ny, FBD, LANES), f32),
            dma((5,)),
            dma,
            dma((scen,)),
            dma((scen, nz)),
            dma((scen, nz)),
            dma((2, len(CHUNKS))),
            dma((2, len(CHUNKS))),
        ]
        + [sems] * 10
        + [dma((2, len(CHUNKS)))],
        compiler_params=pltpu.CompilerParams(
            collective_id=0, has_side_effects=True, vmem_limit_bytes=62 * 2**20
        ),
        name="exchange",
    )(duals, tiles, tile_rows, tile_cols, block_counts.reshape(scen), probabilities, customer_map)
    return pl.pallas_call(
        finish_kernel,
        out_shape=jax.ShapeDtypeStruct(costs.shape, f32),
        in_specs=[vmem, vmem],
        out_specs=hbm,
        scratch_shapes=[pltpu.VMEM(costs.shape, f32), dma((FBD // 8,))],
        compiler_params=pltpu.CompilerParams(vmem_limit_bytes=32 * 2**20),
        name="finish",
    )(costs, gradient)


def solution(mesh):
    nz = mesh.shape["fac"]
    chips = mesh.shape["scen"] // 2
    side = 1
    while side * side < chips:
        side += 1
    in_specs = (
        P("scen", "fac", None),
        P("scen", "fac", None),
        P("scen", "fac"),
        P("scen", "fac"),
        P("scen", "fac"),
        P("scen"),
        P(),
        P("fac", None),
    )
    out_specs = P("fac", None)
    return jax.shard_map(
        functools.partial(local, side, side, nz),
        mesh=mesh,
        in_specs=in_specs,
        out_specs=out_specs,
        check_vma=False,
    )
```

time: 374 us -> 66.3 us (0.18)
  local copies, waits for them, and re-layouts: 147 us -> 1.31 us
  waiting for transfers between devices: 141 us -> 0 us
  Pallas kernels: 0 us -> 64.8 us
  matrix products: 31 us -> 0 us
  other arithmetic: 29.6 us -> 0 us
  between operations: 13.5 us -> 0.03 us
  starting transfers between devices: 9.18 us -> 0 us
    psum x1 -> x0, waiting for transfers between devices: 112 us -> none  [local(): summed = lax.psum(gradient_rows, 'scen')]
    pallas_call x0 -> x2, Pallas kernels: none -> 64.8 us  [the longest x1 62.6 us: local(): pl.pallas_call(functools.partial(exchange_kernel, ny, nx, nz, scen), out_...]
    while x80 -> x0, local copies, waits for them, and re-layouts: 59.4 us -> none
    dot_general x24 -> x0, matrix products: 31 us -> none  [the longest x8 22.2 us: tile_terms(): return folded + jnp.dot(selector, lower, preferred_element_type=jnp.float32)]
    all_to_all x1 -> x0, waiting for transfers between devices: 29.1 us -> none  [local(): lax.all_to_all(outgoing, 'fac', split_axis=1, concat_axis=1, tiled=True)]
    reshape x11 -> x0, local copies, waits for them, and re-layouts: 28.6 us -> none  [the longest x8 23.9 us: tile_terms(): square_set = tile_set.reshape(slot_count, TILE, TILE)]
    dynamic_slice x32 -> x0, local copies, waits for them, and re-layouts: 26.5 us -> none  [local(): lax.scan(scenario_sum, initial, (tiles, tile_rows, tile_cols, block_count...]
    gather x9 -> x0, local copies, waits for them, and re-layouts: 26.2 us -> none  [the longest x8 25.6 us: tile_terms(): jnp.take(block_duals, row_set, axis=0).reshape(slot_count, TILE, periods)]
  transfers between devices with their start and end apart: 2 -> 0, of which waited for: 2 -> 0; matrix products, arithmetic and copies ran while one was open for 0% -> 0% of each run, Pallas kernels for 0% -> 0%
where the time goes in v2:
time: 66.3 us; the launch traced here: 66.2 us
  Pallas kernels  64.8 us (98%)
  local copies, waits for them, and re-layouts  1.31 us (2%)
    pallas_call x1, Pallas kernels, local(): pl.pallas_call(functools.partial(exchange_kernel, ny, nx, nz, scen), out_...  62.6 us
    pallas_call x1, Pallas kernels, local(): pl.pallas_call(finish_kernel, out_shape=jax.ShapeDtypeStruct(costs.shape,...  2.23 us

profile of v2, /device:TPU:1, one launch (start us, length us, event | category | flops | bytes accessed | tf_op | source)
XLA Modules:
  0.0 66.2 jit_solution(18247554118013845199)
XLA Ops:
  0.0 0.0 copy-start.1
  0.0 62.6 %exchange.1.gradient_ref = f32[64,40,128]{2,1,0:T(8,128)} custom-call(bf16[8,512,128]{2,1,0:T(8,128)(2,1)} %duals_hbm.1, bf16[8,128,4096]{2,1,0:T(8,128)(2,1)} %tiles_hbm.1, s32[8,128]{1,0:T(8,128)} %rows_hbm.1, s32[8,128]{1,0:T(8,128)} %cols_hbm.1, s32[8]{0:T(128)} %bitcast.1, f32[8]{0:T(128)} %prob_hbm.1, s32[64]{0:T(128)} %map_hbm.1), custom_call_target="tpu_custom_call" | custom-call | tf_op jit(solution)/shard_map/exchange/pallas_call | solution.py:392
  62.6 0.0 copy-done.1
  62.6 0.0 copy-start
  62.6 1.3 %copy-done = f32[64,40,128]{2,1,0:T(8,128)S(1)} copy-done((f32[64,40,128]{2,1,0:T(8,128)S(1)}, f32[64,40,128]{2,1,0:T(8,128)}, u32[]{:S(2)}) %copy-start) | copy-done | bytes 1310744
  63.9 2.2 %finish.1 = f32[2560,128]{1,0:T(8,128)} custom-call(f32[2560,128]{1,0:T(8,128)S(1)} %copy-done.1, f32[64,40,128]{2,1,0:T(8,128)S(1)} %copy-done), custom_call_target="tpu_custom_call" | custom-call | tf_op jit(solution)/shard_map/finish/pallas_call | solution.py:436
Async XLA Ops:
  0.0 62.6 %copy-start.1 = (f32[2560,128]{1,0:T(8,128)S(1)}, f32[2560,128]{1,0:T(8,128)}, u32[]{:S(2)}) copy-start(f32[2560,128]{1,0:T(8,128)} %costs_ref.1) | copy-start | bytes 3932164
  62.6 1.3 %copy-start = (f32[64,40,128]{2,1,0:T(8,128)S(1)}, f32[64,40,128]{2,1,0:T(8,128)}, u32[]{:S(2)}) copy-start(f32[64,40,128]{2,1,0:T(8,128)} %exchange.1.gradient_ref) | copy-start | bytes 3932164

commit v3 on v2

v3 whole, which is shorter than its diff:
```python
import functools

import jax
import jax.numpy as jnp
from jax import lax
from jax.experimental import pallas as pl
from jax.experimental.pallas import tpu as pltpu
from jax.sharding import PartitionSpec as P

TILE = 64
FBD = 40
SLOTS = 128
LANES = 128
PAIRS = TILE // 2
WIDE = 16
DEEP = 5
TOP = 32767.0
MESH = pl.DeviceIdType.MESH


def coded(value):
    most = jnp.max(jnp.abs(value), axis=0, keepdims=True)
    steps = value * (TOP / jnp.maximum(most, 1e-30))
    return jnp.floor(steps + 0.5).astype(jnp.int32).astype(jnp.int16), most * (1.0 / TOP)


def decoded(steps, scale):
    return steps.astype(jnp.int32).astype(jnp.float32) * scale


def exchange_kernel(
    ny,
    nx,
    nz,
    scen,
    duals_hbm,
    tiles_hbm,
    rows_hbm,
    cols_hbm,
    counts_hbm,
    prob_hbm,
    map_hbm,
    costs_hbm,
    out,
    out_scale,
    rows_ref,
    cols_ref,
    counts_ref,
    prob_ref,
    map_ref,
    duals_v,
    tiles_v,
    stage,
    land,
    selector,
    high,
    low,
    weights,
    acc,
    core_in,
    own_costs,
    r_out,
    r_out_scale,
    r_in,
    r_in_scale,
    last,
    last_scale,
    small_sem,
    duals_sem,
    tiles_sem,
    z_send,
    z_recv,
    c_send,
    c_recv,
    r_send,
    r_recv,
    rs_send,
    rs_recv,
    g_send,
    g_recv,
    gs_send,
    gs_recv,
    f_send,
    f_recv,
    fs_send,
    fs_recv,
    own_sem,
):
    sc = lax.axis_index("scen")
    me = lax.axis_index("fac")
    core = lax.rem(sc, 2)
    xx = lax.rem(lax.div(sc, 2), nx)
    yy = lax.div(sc, 2 * nx)
    chips = ny * nx
    chip = lax.div(sc, 2)

    def at(y, x, c):
        return (lax.rem(y, ny) * nx + lax.rem(x, nx)) * 2 + c

    sibling = (at(yy, xx, 1 - core), me)

    barrier = pltpu.get_barrier_semaphore()
    peers = [(sc, lax.rem(me + d, nz)) for d in range(1, nz)]
    peers += [(at(yy + e // nx, xx + e % nx, core), me) for e in range(1, chips)]
    peers.append(sibling)
    for one in peers:
        pl.semaphore_signal(barrier, inc=1, device_id=one, device_id_type=MESH)

    duals_copy = pltpu.make_async_copy(duals_hbm, duals_v, duals_sem)
    pairs = ((map_hbm, map_ref), (rows_hbm, rows_ref), (cols_hbm, cols_ref), (counts_hbm, counts_ref), (prob_hbm, prob_ref))
    smalls = [pltpu.make_async_copy(src, dst, small_sem.at[n]) for n, (src, dst) in enumerate(pairs)]
    smalls[0].start()
    duals_copy.start()
    for one in smalls[1:]:
        one.start()

    per = PAIRS // chips

    def costs_copy(n):
        j = 2 * (chip * per + n) + core
        return pltpu.make_async_copy(costs_hbm.at[:, j], own_costs.at[n], own_sem.at[2 + n])

    for n in range(per):
        costs_copy(n).start()

    def tiles_copy(s):
        return pltpu.make_async_copy(tiles_hbm.at[s], tiles_v.at[s], tiles_sem.at[s])

    @pl.loop(0, scen)
    def _(s):
        tiles_copy(s).start()

    weights[...] = jnp.zeros_like(weights)
    acc[...] = jnp.zeros_like(acc)
    for one in smalls:
        one.wait()

    owners = [map_ref[me * nz + k] for k in range(nz)]
    keep = [[jnp.where(owner == o, 1.0, 0.0) for owner in owners] for o in range(nz)]
    duals_copy.wait()

    @pl.loop(0, scen)
    def _(s):
        blocks = [duals_v[s, k * TILE : (k + 1) * TILE, :].astype(jnp.float32) for k in range(nz)]
        for o in range(nz):
            block = blocks[0] * keep[o][0]
            for k in range(1, nz):
                block = block + blocks[k] * keep[o][k]
            stage[s, o] = block.astype(jnp.bfloat16)

    def densify(s):
        slot = lax.rem(s, DEEP)
        position = lax.broadcasted_iota(jnp.int32, (1, SLOTS), 1)
        cells = rows_ref[pl.ds(s, 1), :] * FBD + cols_ref[pl.ds(s, 1), :]
        cells = jnp.where(position < counts_ref[s], cells, -1)
        cell_ids = lax.broadcasted_iota(jnp.int32, (nz * FBD, SLOTS), 0)
        selector[...] = jnp.where(cell_ids == cells, 1.0, 0.0).astype(jnp.bfloat16)
        tiles_copy(s).wait()
        for n in range(WIDE):
            block = tiles_v[s, :, n * 256 : (n + 1) * 256]
            dense = jnp.dot(selector[...], block, preferred_element_type=jnp.float32)
            for r in range(nz):
                part = dense[r * FBD : (r + 1) * FBD]
                both = jnp.concatenate([part[:, :LANES], part[:, LANES:]], axis=0)
                upper = both.astype(jnp.bfloat16)
                lower = (both - upper.astype(jnp.float32)).astype(jnp.bfloat16)
                high[slot, n * 80 : (n + 1) * 80, r * LANES : (r + 1) * LANES] = upper
                low[slot, n * 80 : (n + 1) * 80, r * LANES : (r + 1) * LANES] = lower

    densify(0)
    pl.semaphore_wait(barrier, len(peers))

    def z_copy(s, d):
        to = lax.rem(me + d, nz)
        return pltpu.make_async_remote_copy(
            src_ref=stage.at[s, to],
            dst_ref=land.at[s, me],
            send_sem=z_send.at[s, d],
            recv_sem=z_recv.at[s, d],
            device_id=(sc, to),
            device_id_type=MESH,
        )

    def z_arrival(s, d):
        source = lax.rem(me + nz - d, nz)
        return pltpu.make_async_remote_copy(
            src_ref=stage.at[s, source],
            dst_ref=land.at[s, source],
            send_sem=z_send.at[s, d],
            recv_sem=z_recv.at[s, d],
            device_id=(sc, source),
            device_id_type=MESH,
        )

    order = sorted(range(1, nz), key=lambda d: -min(d, nz - d))

    @pl.loop(0, scen)
    def _(s):
        for d in order:
            z_copy(s, d).start()
        land[s, me] = stage[s, me]

    @pl.loop(1, min(DEEP, scen))
    def _(s):
        densify(s)

    part = PAIRS // 2
    mine = core * PAIRS
    other = (1 - core) * PAIRS

    def core_copy(k):
        return pltpu.make_async_remote_copy(
            src_ref=acc.at[pl.ds(other + k * part, part)],
            dst_ref=core_in.at[pl.ds(k * part, part)],
            send_sem=c_send.at[k],
            recv_sem=c_recv.at[k],
            device_id=sibling,
            device_id_type=MESH,
        )

    @pl.loop(0, scen)
    def _(s):
        slot = lax.rem(s, DEEP)
        for d in range(1, nz):
            z_arrival(s, d).wait_recv()
        for r in range(nz):
            block = land[s, r]
            weights[r * LANES : r * LANES + TILE, :LANES] = block
            weights[r * LANES + TILE : (r + 1) * LANES, LANES:] = block

        scale = prob_ref[s]
        for n in range(4):
            rows = slice(n * 320, (n + 1) * 320)
            value = jnp.dot(high[slot, rows], weights[...], preferred_element_type=jnp.float32)
            value = value + jnp.dot(low[slot, rows], weights[...], preferred_element_type=jnp.float32)
            value = value * scale
            acc[n * 8 : (n + 1) * 8] += value[:, :LANES].reshape(8, FBD, LANES)
            acc[PAIRS + n * 8 : PAIRS + (n + 1) * 8] += value[:, LANES:].reshape(8, FBD, LANES)
            if n % 2:

                @pl.when(s == scen - 1)
                def _():
                    core_copy(n // 2).start()

        @pl.when(s < scen - DEEP)
        def _():
            densify(s + DEEP)

    def remote(src, dst, send, recv, to):
        return pltpu.make_async_remote_copy(
            src_ref=src, dst_ref=dst, send_sem=send, recv_sem=recv, device_id=to, device_id_type=MESH
        )

    def there(e):
        return lax.rem(yy + e // nx, ny) * nx + lax.rem(xx + e % nx, nx)

    def whence(e):
        return lax.rem(yy + ny - e // nx, ny) * nx + lax.rem(xx + nx - e % nx, nx)

    def r_copies(e):
        to = there(e)
        device = (to * 2 + core, me)
        return (
            remote(r_out.at[to], r_in.at[e], r_send.at[e], r_recv.at[e], device),
            remote(r_out_scale.at[to], r_in_scale.at[e], rs_send.at[e], rs_recv.at[e], device),
        )

    def g_copies(e, shard):
        device = (there(e) * 2 + core, me)
        return (
            remote(last, out.at[shard], g_send.at[e], g_recv.at[e], device),
            remote(last_scale, out_scale.at[shard], gs_send.at[e], gs_recv.at[e], device),
        )

    def f_copies(e, shard):
        return (
            remote(out.at[shard], out.at[shard], f_send.at[e], f_recv.at[e], sibling),
            remote(out_scale.at[shard], out_scale.at[shard], fs_send.at[e], fs_recv.at[e], sibling),
        )

    hops = sorted(range(1, chips), key=lambda e: -min(e // nx, ny - e // nx) - min(e % nx, nx - e % nx))
    own = (
        pltpu.make_async_copy(last, out.at[core * chips + chip], own_sem.at[0]),
        pltpu.make_async_copy(last_scale, out_scale.at[core * chips + chip], own_sem.at[1]),
    )
    rows = per * FBD

    def wide(scale):
        return jnp.broadcast_to(scale, (8, LANES))

    for k in range(2):
        core_copy(k).wait_recv()
    for e in hops:
        to = there(e)
        value = acc[pl.ds(mine + to * per, per)] + core_in[pl.ds(to * per, per)]
        steps, scale = coded(value.reshape(rows, LANES))
        r_out[to] = steps
        r_out_scale[to] = wide(scale)
        for one in r_copies(e):
            one.start()
    total = acc[pl.ds(mine + chip * per, per)] + core_in[pl.ds(chip * per, per)]
    total = total.reshape(rows, LANES)
    for n in range(per):
        costs_copy(n).wait()
    for e in hops:
        for one in r_copies(e):
            one.wait_recv()
        total = total + decoded(r_in[e], r_in_scale[e, :1])
    steps, scale = coded(own_costs[...].reshape(rows, LANES) - total)
    last[...] = steps
    last_scale[...] = wide(scale)
    for e in hops:
        for one in g_copies(e, core * chips + chip):
            one.start()
    for one in own:
        one.start()
    for one in own:
        one.wait()
    for one in f_copies(0, core * chips + chip):
        one.start()
    for e in reversed(hops):
        shard = core * chips + whence(e)
        for one in g_copies(e, shard):
            one.wait_recv()
        for one in f_copies(e, shard):
            one.start()

    @pl.loop(0, scen)
    def _(s):
        for d in range(1, nz):
            z_copy(s, d).wait_send()

    for k in range(2):
        core_copy(k).wait_send()
    for e in hops:
        for one in r_copies(e) + g_copies(e, core * chips + chip):
            one.wait_send()
    for e in range(chips):
        shard = whence(e)
        for one in f_copies(e, core * chips + shard):
            one.wait_send()
        for one in f_copies(e, (1 - core) * chips + shard):
            one.wait_recv()


def finish_kernel(steps_ref, scale_ref, out_ref):
    shards = steps_ref.shape[0] // 2
    per = PAIRS // shards
    for q in range(2 * shards):
        value = decoded(steps_ref[q], scale_ref[q, :1])
        for n in range(per):
            j = 2 * ((q % shards) * per + n) + q // shards
            out_ref[pl.ds(j, FBD, stride=TILE), :] = value[n * FBD : (n + 1) * FBD]


def local(ny, nx, nz, duals, tiles, tile_rows, tile_cols, block_counts, probabilities, customer_map, costs):
    scen = duals.shape[0]
    bf16, f32 = jnp.bfloat16, jnp.float32
    chips = ny * nx
    rows = PAIRS // chips * FBD
    i16 = jnp.int16
    vmem = pl.BlockSpec(memory_space=pltpu.VMEM)
    far = pl.BlockSpec(memory_space=pl.ANY)
    hbm = pl.BlockSpec(memory_space=pltpu.HBM)
    dma = pltpu.SemaphoreType.DMA
    sems = dma((chips,))
    deep = min(DEEP, scen)
    steps, scale = pl.pallas_call(
        functools.partial(exchange_kernel, ny, nx, nz, scen),
        out_shape=(
            jax.ShapeDtypeStruct((2 * chips, rows, LANES), i16),
            jax.ShapeDtypeStruct((2 * chips, 8, LANES), f32),
        ),
        in_specs=[hbm] * 8,
        out_specs=(far, far),
        scratch_shapes=[
            pltpu.VMEM(tile_rows.shape, jnp.int32),
            pltpu.VMEM(tile_cols.shape, jnp.int32),
            pltpu.SMEM((scen,), jnp.int32),
            pltpu.SMEM((scen,), f32),
            pltpu.SMEM(customer_map.shape, jnp.int32),
            pltpu.VMEM(duals.shape, bf16),
            pltpu.VMEM(tiles.shape, bf16),
            pltpu.VMEM((scen, nz, TILE, LANES), bf16),
            pltpu.VMEM((scen, nz, TILE, LANES), bf16),
            pltpu.VMEM((nz * FBD, SLOTS), bf16),
            pltpu.VMEM((deep, PAIRS * FBD, nz * LANES), bf16),
            pltpu.VMEM((deep, PAIRS * FBD, nz * LANES), bf16),
            pltpu.VMEM((nz * LANES, 2 * LANES), bf16),
            pltpu.VMEM((TILE, FBD, LANES), f32),
            pltpu.VMEM((PAIRS, FBD, LANES), f32),
            pltpu.VMEM((PAIRS // chips, FBD, LANES), f32),
            pltpu.VMEM((chips, rows, LANES), i16),
            pltpu.VMEM((chips, 8, LANES), f32),
            pltpu.VMEM((chips, rows, LANES), i16),
            pltpu.VMEM((chips, 8, LANES), f32),
            pltpu.VMEM((rows, LANES), i16),
            pltpu.VMEM((8, LANES), f32),
            dma((5,)),
            dma,
            dma((scen,)),
            dma((scen, nz)),
            dma((scen, nz)),
            dma((2,)),
            dma((2,)),
        ]
        + [sems] * 12
        + [dma((2 + PAIRS // chips,))],
        compiler_params=pltpu.CompilerParams(
            collective_id=0, has_side_effects=True, vmem_limit_bytes=62 * 2**20
        ),
        name="exchange",
    )(duals, tiles, tile_rows, tile_cols, block_counts.reshape(scen), probabilities, customer_map, costs.reshape(FBD, TILE, LANES))
    return pl.pallas_call(
        finish_kernel,
        out_shape=jax.ShapeDtypeStruct(costs.shape, f32),
        in_specs=[vmem, vmem],
        out_specs=vmem,
        compiler_params=pltpu.CompilerParams(vmem_limit_bytes=32 * 2**20),
        name="finish",
    )(steps, scale)


def solution(mesh):
    nz = mesh.shape["fac"]
    chips = mesh.shape["scen"] // 2
    side = 1
    while side * side < chips:
        side += 1
    in_specs = (
        P("scen", "fac", None),
        P("scen", "fac", None),
        P("scen", "fac"),
        P("scen", "fac"),
        P("scen", "fac"),
        P("scen"),
        P(),
        P("fac", None),
    )
    out_specs = P("fac", None)
    return jax.shard_map(
        functools.partial(local, side, side, nz),
        mesh=mesh,
        in_specs=in_specs,
        out_specs=out_specs,
        check_vma=False,
    )
```

time: 66.3 us -> 62.8 us (0.947)
  Pallas kernels: 64.8 us -> 60.6 us
  local copies, waits for them, and re-layouts: 1.31 us -> 1.98 us
    pallas_call x1, Pallas kernels: 62.6 us -> 58.3 us  [local(): pl.pallas_call(functools.partial(exchange_kernel, ny, nx, nz, scen), out_...]
    unnamed x4, local copies, waits for them, and re-layouts: 1.31 us -> 1.98 us
where the time goes in v3:
time: 62.8 us; the launch traced here: 62.6 us
  Pallas kernels  60.6 us (96%)
  local copies, waits for them, and re-layouts  1.98 us (3%)
    pallas_call x1, Pallas kernels, local(): pl.pallas_call(functools.partial(exchange_kernel, ny, nx, nz, scen), out_...  58.3 us
    pallas_call x1, Pallas kernels, local(): pl.pallas_call(finish_kernel, out_shape=jax.ShapeDtypeStruct(costs.shape,...  2.31 us
    unnamed x4, local copies, waits for them, and re-layouts  1.98 us

profile of v3, /device:TPU:1, one launch (start us, length us, event | category | flops | bytes accessed | tf_op | source)
XLA Modules:
  0.0 62.6 jit_solution(16825198435547227505)
XLA Ops:
  0.0 58.3 %exchange.1 = (s16[32,80,128]{2,1,0:T(8,128)(2,1)}, f32[32,8,128]{2,1,0:T(8,128)}) custom-call(bf16[8,512,128]{2,1,0:T(8,128)(2,1)} %duals_hbm.1, bf16[8,128,4096]{2,1,0:T(8,128)(2,1)} %tiles_hbm.1, s32[8,128]{1,0:T(8,128)} %rows_hbm.1, s32[8,128]{1,0:T(8,128)} %cols_hbm.1, s32[8]{0:T(128)} %bitcast.3, f32[8]{0:T(128)} %prob_hbm.1, s32[64]{0:T(128)} %map_hbm.1, ...), custom_call_target="tpu_custom_call" | custom-call | tf_op jit(solution)/shard_map/exchange/pallas_call | solution.py:368
  58.3 0.0 copy-start
  58.3 1.1 %copy-done = s16[32,80,128]{2,1,0:T(8,128)(2,1)S(1)} copy-done((s16[32,80,128]{2,1,0:T(8,128)(2,1)S(1)}, s16[32,80,128]{2,1,0:T(8,128)(2,1)}, u32[]{:S(2)}) %copy-start) | copy-done | bytes 655384
  59.4 0.0 copy-start.1
  59.4 0.9 %copy-done.1 = f32[32,8,128]{2,1,0:T(8,128)S(1)} copy-done((f32[32,8,128]{2,1,0:T(8,128)S(1)}, f32[32,8,128]{2,1,0:T(8,128)}, u32[]{:S(2)}) %copy-start.1) | copy-done | bytes 131096
  60.3 2.3 %finish.1 = f32[2560,128]{1,0:T(8,128)} custom-call(s16[32,80,128]{2,1,0:T(8,128)(2,1)S(1)} %copy-done, f32[32,8,128]{2,1,0:T(8,128)S(1)} %copy-done.1), custom_call_target="tpu_custom_call" | custom-call | tf_op jit(solution)/shard_map/finish/pallas_call | solution.py:414
Async XLA Ops:
  58.3 1.1 %copy-start = (s16[32,80,128]{2,1,0:T(8,128)(2,1)S(1)}, s16[32,80,128]{2,1,0:T(8,128)(2,1)}, u32[]{:S(2)}) copy-start(s16[32,80,128]{2,1,0:T(8,128)(2,1)} %get-tuple-element.7.steps_ref) | copy-start | bytes 1966084
  59.4 0.9 %copy-start.1 = (f32[32,8,128]{2,1,0:T(8,128)S(1)}, f32[32,8,128]{2,1,0:T(8,128)}, u32[]{:S(2)}) copy-start(f32[32,8,128]{2,1,0:T(8,128)} %get-tuple-element.8.scale_ref) | copy-start | bytes 393220

commit v4 on v3

--- a/solution.py
+++ b/solution.py
@@ -14,18 +14,23 @@
 PAIRS = TILE // 2
 WIDE = 16
 DEEP = 5
-TOP = 32767.0
+TOP = 32000.0
+MARK = 16
+GROUP = 5
 MESH = pl.DeviceIdType.MESH
 
 
 def coded(value):
     most = jnp.max(jnp.abs(value), axis=0, keepdims=True)
-    steps = value * (TOP / jnp.maximum(most, 1e-30))
-    return jnp.floor(steps + 0.5).astype(jnp.int32).astype(jnp.int16), most * (1.0 / TOP)
-
-
-def decoded(steps, scale):
-    return steps.astype(jnp.int32).astype(jnp.float32) * scale
+    power = jnp.ceil(jnp.log2(jnp.maximum(most, 1e-30)))
+    steps = jnp.floor(value * (jnp.exp2(-power) * TOP) + 0.5)
+    mark = jnp.broadcast_to(power, (MARK, LANES))
+    return jnp.concatenate([steps, mark], axis=0).astype(jnp.int32).astype(jnp.int16)
+
+
+def decoded(message):
+    wide = message.astype(jnp.int32).astype(jnp.float32)
+    return wide[:-MARK] * (jnp.exp2(wide[-MARK : 1 - MARK]) * (1.0 / TOP))
 
 
 def exchange_kernel(
@@ -41,8 +46,7 @@
     prob_hbm,
     map_hbm,
     costs_hbm,
-    out,
-    out_scale,
+    out_hbm,
     rows_ref,
     cols_ref,
     counts_ref,
@@ -60,11 +64,10 @@
     core_in,
     own_costs,
     r_out,
-    r_out_scale,
     r_in,
-    r_in_scale,
     last,
-    last_scale,
+    gathered,
+    out_v,
     small_sem,
     duals_sem,
     tiles_sem,
@@ -74,17 +77,12 @@
     c_recv,
     r_send,
     r_recv,
-    rs_send,
-    rs_recv,
     g_send,
     g_recv,
-    gs_send,
-    gs_recv,
     f_send,
     f_recv,
-    fs_send,
-    fs_recv,
     own_sem,
+    out_sem,
 ):
     sc = lax.axis_index("scen")
     me = lax.axis_index("fac")
@@ -118,7 +116,7 @@
 
     def costs_copy(n):
         j = 2 * (chip * per + n) + core
-        return pltpu.make_async_copy(costs_hbm.at[:, j], own_costs.at[n], own_sem.at[2 + n])
+        return pltpu.make_async_copy(costs_hbm.at[:, j], own_costs.at[n], own_sem.at[n])
 
     for n in range(per):
         costs_copy(n).start()
@@ -204,7 +202,7 @@
     def _(s):
         densify(s)
 
-    part = PAIRS // 2
+    part = PAIRS // 4
     mine = core * PAIRS
     other = (1 - core) * PAIRS
 
@@ -236,11 +234,10 @@
             value = value * scale
             acc[n * 8 : (n + 1) * 8] += value[:, :LANES].reshape(8, FBD, LANES)
             acc[PAIRS + n * 8 : PAIRS + (n + 1) * 8] += value[:, LANES:].reshape(8, FBD, LANES)
-            if n % 2:
-
-                @pl.when(s == scen - 1)
-                def _():
-                    core_copy(n // 2).start()
+
+            @pl.when(s == scen - 1)
+            def _():
+                core_copy(n).start()
 
         @pl.when(s < scen - DEEP)
         def _():
@@ -257,100 +254,73 @@
     def whence(e):
         return lax.rem(yy + ny - e // nx, ny) * nx + lax.rem(xx + nx - e % nx, nx)
 
-    def r_copies(e):
+    def r_copy(e):
         to = there(e)
-        device = (to * 2 + core, me)
-        return (
-            remote(r_out.at[to], r_in.at[e], r_send.at[e], r_recv.at[e], device),
-            remote(r_out_scale.at[to], r_in_scale.at[e], rs_send.at[e], rs_recv.at[e], device),
-        )
-
-    def g_copies(e, shard):
-        device = (there(e) * 2 + core, me)
-        return (
-            remote(last, out.at[shard], g_send.at[e], g_recv.at[e], device),
-            remote(last_scale, out_scale.at[shard], gs_send.at[e], gs_recv.at[e], device),
-        )
-
-    def f_copies(e, shard):
-        return (
-            remote(out.at[shard], out.at[shard], f_send.at[e], f_recv.at[e], sibling),
-            remote(out_scale.at[shard], out_scale.at[shard], fs_send.at[e], fs_recv.at[e], sibling),
-        )
+        return remote(r_out.at[to], r_in.at[e], r_send.at[e], r_recv.at[e], (to * 2 + core, me))
+
+    def g_copy(e, shard):
+        return remote(last, gathered.at[shard], g_send.at[e], g_recv.at[e], (there(e) * 2 + core, me))
+
+    def f_copy(e, src, shard):
+        return remote(src, gathered.at[shard], f_send.at[e], f_recv.at[e], sibling)
 
     hops = sorted(range(1, chips), key=lambda e: -min(e // nx, ny - e // nx) - min(e % nx, nx - e % nx))
-    own = (
-        pltpu.make_async_copy(last, out.at[core * chips + chip], own_sem.at[0]),
-        pltpu.make_async_copy(last_scale, out_scale.at[core * chips + chip], own_sem.at[1]),
-    )
     rows = per * FBD
 
-    def wide(scale):
-        return jnp.broadcast_to(scale, (8, LANES))
-
-    for k in range(2):
+    def place(message, half, where):
+        value = decoded(message)
+        for n in range(per):
+            j = 2 * (where * per + n) + half
+            out_v[pl.ds(j, FBD, stride=TILE), :] = value[n * FBD : (n + 1) * FBD]
+
+    for k in range(4):
         core_copy(k).wait_recv()
-    for e in hops:
-        to = there(e)
-        value = acc[pl.ds(mine + to * per, per)] + core_in[pl.ds(to * per, per)]
-        steps, scale = coded(value.reshape(rows, LANES))
-        r_out[to] = steps
-        r_out_scale[to] = wide(scale)
-        for one in r_copies(e):
-            one.start()
+    for first in range(0, chips - 1, GROUP):
+        group = hops[first : first + GROUP]
+        values = [acc[pl.ds(mine + there(e) * per, per)] + core_in[pl.ds(there(e) * per, per)] for e in group]
+        messages = [coded(value.reshape(rows, LANES)) for value in values]
+        for e, message in zip(group, messages):
+            r_out[there(e)] = message
+        for e in group:
+            r_copy(e).start()
     total = acc[pl.ds(mine + chip * per, per)] + core_in[pl.ds(chip * per, per)]
-    total = total.reshape(rows, LANES)
     for n in range(per):
         costs_copy(n).wait()
+    total = (own_costs[...] - total).reshape(rows, LANES)
     for e in hops:
-        for one in r_copies(e):
-            one.wait_recv()
-        total = total + decoded(r_in[e], r_in_scale[e, :1])
-    steps, scale = coded(own_costs[...].reshape(rows, LANES) - total)
-    last[...] = steps
-    last_scale[...] = wide(scale)
+        r_copy(e).wait_recv()
+        total = total - decoded(r_in[e])
+    shard = core * chips + chip
+    last[...] = coded(total)
     for e in hops:
-        for one in g_copies(e, core * chips + chip):
-            one.start()
-    for one in own:
-        one.start()
-    for one in own:
-        one.wait()
-    for one in f_copies(0, core * chips + chip):
-        one.start()
+        g_copy(e, shard).start()
+    f_copy(0, last, shard).start()
+    place(last[...], core, chip)
     for e in reversed(hops):
         shard = core * chips + whence(e)
-        for one in g_copies(e, shard):
-            one.wait_recv()
-        for one in f_copies(e, shard):
-            one.start()
+        g_copy(e, shard).wait_recv()
+        f_copy(e, gathered.at[shard], shard).start()
+        place(gathered[shard], core, whence(e))
+    for e in [0] + hops[::-1]:
+        shard = (1 - core) * chips + whence(e)
+        f_copy(e, last, shard).wait_recv()
+        place(gathered[shard], 1 - core, whence(e))
+    out_copy = pltpu.make_async_copy(out_v, out_hbm, out_sem)
+    out_copy.start()
 
     @pl.loop(0, scen)
     def _(s):
         for d in range(1, nz):
             z_copy(s, d).wait_send()
 
-    for k in range(2):
+    for k in range(4):
         core_copy(k).wait_send()
     for e in hops:
-        for one in r_copies(e) + g_copies(e, core * chips + chip):
-            one.wait_send()
+        r_copy(e).wait_send()
+        g_copy(e, core * chips + chip).wait_send()
     for e in range(chips):
-        shard = whence(e)
-        for one in f_copies(e, core * chips + shard):
-            one.wait_send()
-        for one in f_copies(e, (1 - core) * chips + shard):
-            one.wait_recv()
-
-
-def finish_kernel(steps_ref, scale_ref, out_ref):
-    shards = steps_ref.shape[0] // 2
-    per = PAIRS // shards
-    for q in range(2 * shards):
-        value = decoded(steps_ref[q], scale_ref[q, :1])
-        for n in range(per):
-            j = 2 * ((q % shards) * per + n) + q // shards
-            out_ref[pl.ds(j, FBD, stride=TILE), :] = value[n * FBD : (n + 1) * FBD]
+        f_copy(e, last, core * chips + chip).wait_send()
+    out_copy.wait()
 
 
 def local(ny, nx, nz, duals, tiles, tile_rows, tile_cols, block_counts, probabilities, customer_map, costs):
@@ -359,20 +329,15 @@
     chips = ny * nx
     rows = PAIRS // chips * FBD
     i16 = jnp.int16
-    vmem = pl.BlockSpec(memory_space=pltpu.VMEM)
-    far = pl.BlockSpec(memory_space=pl.ANY)
     hbm = pl.BlockSpec(memory_space=pltpu.HBM)
     dma = pltpu.SemaphoreType.DMA
     sems = dma((chips,))
     deep = min(DEEP, scen)
-    steps, scale = pl.pallas_call(
+    return pl.pallas_call(
         functools.partial(exchange_kernel, ny, nx, nz, scen),
-        out_shape=(
-            jax.ShapeDtypeStruct((2 * chips, rows, LANES), i16),
-            jax.ShapeDtypeStruct((2 * chips, 8, LANES), f32),
-        ),
+        out_shape=jax.ShapeDtypeStruct(costs.shape, f32),
         in_specs=[hbm] * 8,
-        out_specs=(far, far),
+        out_specs=hbm,
         scratch_shapes=[
             pltpu.VMEM(tile_rows.shape, jnp.int32),
             pltpu.VMEM(tile_cols.shape, jnp.int32),
@@ -390,35 +355,26 @@
             pltpu.VMEM((TILE, FBD, LANES), f32),
             pltpu.VMEM((PAIRS, FBD, LANES), f32),
             pltpu.VMEM((PAIRS // chips, FBD, LANES), f32),
-            pltpu.VMEM((chips, rows, LANES), i16),
-            pltpu.VMEM((chips, 8, LANES), f32),
-            pltpu.VMEM((chips, rows, LANES), i16),
-            pltpu.VMEM((chips, 8, LANES), f32),
-            pltpu.VMEM((rows, LANES), i16),
-            pltpu.VMEM((8, LANES), f32),
+            pltpu.VMEM((chips, rows + MARK, LANES), i16),
+            pltpu.VMEM((chips, rows + MARK, LANES), i16),
+            pltpu.VMEM((rows + MARK, LANES), i16),
+            pltpu.VMEM((2 * chips, rows + MARK, LANES), i16),
+            pltpu.VMEM(costs.shape, f32),
             dma((5,)),
             dma,
             dma((scen,)),
             dma((scen, nz)),
             dma((scen, nz)),
-            dma((2,)),
-            dma((2,)),
+            dma((4,)),
+            dma((4,)),
         ]
-        + [sems] * 12
-        + [dma((2 + PAIRS // chips,))],
+        + [sems] * 6
+        + [dma((PAIRS // chips,)), dma],
         compiler_params=pltpu.CompilerParams(
             collective_id=0, has_side_effects=True, vmem_limit_bytes=62 * 2**20
         ),
         name="exchange",
     )(duals, tiles, tile_rows, tile_cols, block_counts.reshape(scen), probabilities, customer_map, costs.reshape(FBD, TILE, LANES))
-    return pl.pallas_call(
-        finish_kernel,
-        out_shape=jax.ShapeDtypeStruct(costs.shape, f32),
-        in_specs=[vmem, vmem],
-        out_specs=vmem,
-        compiler_params=pltpu.CompilerParams(vmem_limit_bytes=32 * 2**20),
-        name="finish",
-    )(steps, scale)
 
 
 def solution(mesh):

time: 62.8 us -> 72.1 us (1.15)
  Pallas kernels: 60.6 us -> 69.5 us
    pallas_call x1, Pallas kernels: 58.3 us -> 69.5 us  [local(): pl.pallas_call(functools.partial(exchange_kernel, ny, nx, nz, scen), out_...]
    pallas_call x1 -> x0, Pallas kernels: 2.31 us -> none  [local(): pl.pallas_call(finish_kernel, out_shape=jax.ShapeDtypeStruct(costs.shape,...]
    unnamed x4 -> x1, local copies, waits for them, and re-layouts: 1.98 us -> 2.46 us
where the time goes in v4:
time: 72.1 us; the launch traced here: 72 us
  Pallas kernels  69.5 us (96%)
  local copies, waits for them, and re-layouts  2.46 us (3%)
    pallas_call x1, Pallas kernels, local(): pl.pallas_call(functools.partial(exchange_kernel, ny, nx, nz, scen), out_...  69.5 us
    unnamed x1, local copies, waits for them, and re-layouts  2.46 us

profile of v4, /device:TPU:1, one launch (start us, length us, event | category | flops | bytes accessed | tf_op | source)
XLA Modules:
  0.0 72.0 jit_solution(8420934760614838616)
XLA Ops:
  0.0 69.5 %exchange.1 = f32[2560,128]{1,0:T(8,128)} custom-call(bf16[8,512,128]{2,1,0:T(8,128)(2,1)} %duals_hbm.1, bf16[8,128,4096]{2,1,0:T(8,128)(2,1)} %tiles_hbm.1, s32[8,128]{1,0:T(8,128)} %rows_hbm.1, s32[8,128]{1,0:T(8,128)} %cols_hbm.1, s32[8]{0:T(128)} %bitcast.3, f32[8]{0:T(128)} %prob_hbm.1, s32[64]{0:T(128)} %map_hbm.1, f32[40,64,128]{2,1,0:T(8,128)} %bitcast.2), custom_call_target="tpu_custom_call" | custom-call | tf_op jit(solution)/shard_map/exchange/pallas_call | solution.py:336
  69.5 2.5 %copy.10 = f32[2560,128]{1,0:T(8,128)} copy(f32[2560,128]{1,0:T(8,128)} %exchange.1) | data formatting | bytes 2621440

commit v5 on v4

--- a/solution.py
+++ b/solution.py
@@ -31,6 +31,11 @@
 def decoded(message):
     wide = message.astype(jnp.int32).astype(jnp.float32)
     return wide[:-MARK] * (jnp.exp2(wide[-MARK : 1 - MARK]) * (1.0 / TOP))
+
+
+def by_eight(value):
+    count = value.shape[0]
+    return jnp.concatenate([value[m, c : c + 8] for c in range(0, FBD, 8) for m in range(count)], axis=0)
 
 
 def exchange_kernel(
@@ -46,7 +51,7 @@
     prob_hbm,
     map_hbm,
     costs_hbm,
-    out_hbm,
+    out,
     rows_ref,
     cols_ref,
     counts_ref,
@@ -67,7 +72,6 @@
     r_in,
     last,
     gathered,
-    out_v,
     small_sem,
     duals_sem,
     tiles_sem,
@@ -202,7 +206,7 @@
     def _(s):
         densify(s)
 
-    part = PAIRS // 4
+    part = PAIRS // 2
     mine = core * PAIRS
     other = (1 - core) * PAIRS
 
@@ -234,10 +238,11 @@
             value = value * scale
             acc[n * 8 : (n + 1) * 8] += value[:, :LANES].reshape(8, FBD, LANES)
             acc[PAIRS + n * 8 : PAIRS + (n + 1) * 8] += value[:, LANES:].reshape(8, FBD, LANES)
-
-            @pl.when(s == scen - 1)
-            def _():
-                core_copy(n).start()
+            if n % 2:
+
+                @pl.when(s == scen - 1)
+                def _():
+                    core_copy(n // 2).start()
 
         @pl.when(s < scen - DEEP)
         def _():
@@ -262,23 +267,18 @@
         return remote(last, gathered.at[shard], g_send.at[e], g_recv.at[e], (there(e) * 2 + core, me))
 
     def f_copy(e, src, shard):
-        return remote(src, gathered.at[shard], f_send.at[e], f_recv.at[e], sibling)
+        return remote(src, out.at[shard], f_send.at[e], f_recv.at[e], sibling)
+
+    def out_copy(e, src, shard):
+        return pltpu.make_async_copy(src, out.at[shard], out_sem.at[e])
 
     hops = sorted(range(1, chips), key=lambda e: -min(e // nx, ny - e // nx) - min(e % nx, nx - e % nx))
-    rows = per * FBD
-
-    def place(message, half, where):
-        value = decoded(message)
-        for n in range(per):
-            j = 2 * (where * per + n) + half
-            out_v[pl.ds(j, FBD, stride=TILE), :] = value[n * FBD : (n + 1) * FBD]
-
-    for k in range(4):
+    for k in range(2):
         core_copy(k).wait_recv()
     for first in range(0, chips - 1, GROUP):
         group = hops[first : first + GROUP]
         values = [acc[pl.ds(mine + there(e) * per, per)] + core_in[pl.ds(there(e) * per, per)] for e in group]
-        messages = [coded(value.reshape(rows, LANES)) for value in values]
+        messages = [coded(by_eight(value)) for value in values]
         for e, message in zip(group, messages):
             r_out[there(e)] = message
         for e in group:
@@ -286,7 +286,7 @@
     total = acc[pl.ds(mine + chip * per, per)] + core_in[pl.ds(chip * per, per)]
     for n in range(per):
         costs_copy(n).wait()
-    total = (own_costs[...] - total).reshape(rows, LANES)
+    total = by_eight(own_costs[...] - total)
     for e in hops:
         r_copy(e).wait_recv()
         total = total - decoded(r_in[e])
@@ -295,32 +295,60 @@
     for e in hops:
         g_copy(e, shard).start()
     f_copy(0, last, shard).start()
-    place(last[...], core, chip)
+    out_copy(0, last, shard).start()
     for e in reversed(hops):
         shard = core * chips + whence(e)
         g_copy(e, shard).wait_recv()
         f_copy(e, gathered.at[shard], shard).start()
-        place(gathered[shard], core, whence(e))
-    for e in [0] + hops[::-1]:
-        shard = (1 - core) * chips + whence(e)
-        f_copy(e, last, shard).wait_recv()
-        place(gathered[shard], 1 - core, whence(e))
-    out_copy = pltpu.make_async_copy(out_v, out_hbm, out_sem)
-    out_copy.start()
+        out_copy(e, gathered.at[shard], shard).start()
 
     @pl.loop(0, scen)
     def _(s):
         for d in range(1, nz):
             z_copy(s, d).wait_send()
 
-    for k in range(4):
+    for k in range(2):
         core_copy(k).wait_send()
     for e in hops:
         r_copy(e).wait_send()
         g_copy(e, core * chips + chip).wait_send()
     for e in range(chips):
-        f_copy(e, last, core * chips + chip).wait_send()
-    out_copy.wait()
+        f_copy(e, last, core * chips + whence(e)).wait_send()
+        out_copy(e, last, core * chips + whence(e)).wait()
+        f_copy(e, last, (1 - core) * chips + whence(e)).wait_recv()
+
+
+def finish_kernel(messages, out_hbm, held, out_v, in_sem, out_sem):
+    shards = held.shape[0] // 2
+    per = PAIRS // shards
+    step = 8 * per
+
+    def load(g):
+        rows = pl.ds(g * step, step if g < FBD // 8 else MARK)
+        return pltpu.make_async_copy(messages.at[:, rows], held.at[:, rows], in_sem.at[g])
+
+    def store(g):
+        rows = pl.ds(g * 8 * TILE, 8 * TILE)
+        return pltpu.make_async_copy(out_v.at[rows], out_hbm.at[rows], out_sem.at[g])
+
+    load(FBD // 8).start()
+    for g in range(FBD // 8):
+        load(g).start()
+    load(FBD // 8).wait()
+    scales = []
+    for q in range(2 * shards):
+        mark = held[q, FBD * per : FBD * per + MARK].astype(jnp.int32).astype(jnp.float32)
+        scales.append(jnp.exp2(mark[:1]) * (1.0 / TOP))
+    for g in range(FBD // 8):
+        load(g).wait()
+        for q in range(2 * shards):
+            value = held[q, g * step : (g + 1) * step].astype(jnp.int32).astype(jnp.float32) * scales[q]
+            for n in range(per):
+                j = 2 * ((q % shards) * per + n) + q // shards
+                out_v[pl.ds(g * 8 * TILE + j, 8, stride=TILE), :] = value[n * 8 : (n + 1) * 8]
+        store(g).start()
+    for g in range(FBD // 8):
+        store(g).wait()
 
 
 def local(ny, nx, nz, duals, tiles, tile_rows, tile_cols, block_counts, probabilities, customer_map, costs):
@@ -333,9 +361,9 @@
     dma = pltpu.SemaphoreType.DMA
     sems = dma((chips,))
     deep = min(DEEP, scen)
-    return pl.pallas_call(
+    messages = pl.pallas_call(
         functools.partial(exchange_kernel, ny, nx, nz, scen),
-        out_shape=jax.ShapeDtypeStruct(costs.shape, f32),
+        out_shape=jax.ShapeDtypeStruct((2 * chips, rows + MARK, LANES), i16),
         in_specs=[hbm] * 8,
         out_specs=hbm,
         scratch_shapes=[
@@ -359,22 +387,35 @@
             pltpu.VMEM((chips, rows + MARK, LANES), i16),
             pltpu.VMEM((rows + MARK, LANES), i16),
             pltpu.VMEM((2 * chips, rows + MARK, LANES), i16),
-            pltpu.VMEM(costs.shape, f32),
             dma((5,)),
             dma,
             dma((scen,)),
             dma((scen, nz)),
             dma((scen, nz)),
-            dma((4,)),
-            dma((4,)),
+            dma((2,)),
+            dma((2,)),
         ]
         + [sems] * 6
-        + [dma((PAIRS // chips,)), dma],
+        + [dma((PAIRS // chips,)), sems],
         compiler_params=pltpu.CompilerParams(
             collective_id=0, has_side_effects=True, vmem_limit_bytes=62 * 2**20
         ),
         name="exchange",
     )(duals, tiles, tile_rows, tile_cols, block_counts.reshape(scen), probabilities, customer_map, costs.reshape(FBD, TILE, LANES))
+    return pl.pallas_call(
+        finish_kernel,
+        out_shape=jax.ShapeDtypeStruct(costs.shape, f32),
+        in_specs=[hbm],
+        out_specs=hbm,
+        scratch_shapes=[
+            pltpu.VMEM(messages.shape, i16),
+            pltpu.VMEM(costs.shape, f32),
+            dma((FBD // 8 + 1,)),
+            dma((FBD // 8,)),
+        ],
+        compiler_params=pltpu.CompilerParams(vmem_limit_bytes=62 * 2**20),
+        name="finish",
+    )(messages)
 
 
 def solution(mesh):

time: 72.1 us -> 59.8 us (0.83)
  Pallas kernels: 69.5 us -> 59.7 us
  local copies, waits for them, and re-layouts: 2.46 us -> 0 us
    pallas_call x1, Pallas kernels: 69.5 us -> 57.2 us  [local(): pl.pallas_call(functools.partial(exchange_kernel, ny, nx, nz, scen), out_...]
    pallas_call x0 -> x1, Pallas kernels: none -> 2.58 us  [local(): pl.pallas_call(finish_kernel, out_shape=jax.ShapeDtypeStruct(costs.shape,...]
    unnamed x1 -> x0, local copies, waits for them, and re-layouts: 2.46 us -> none
where the time goes in v5:
time: 59.8 us
  Pallas kernels  59.7 us (100%)
    pallas_call x1, Pallas kernels, local(): pl.pallas_call(functools.partial(exchange_kernel, ny, nx, nz, scen), out_...  57.2 us
    pallas_call x1, Pallas kernels, local(): pl.pallas_call(finish_kernel, out_shape=jax.ShapeDtypeStruct(costs.shape,...  2.58 us

profile of v5, /device:TPU:1, one launch (start us, length us, event | category | flops | bytes accessed | tf_op | source)
XLA Modules:
  0.0 59.8 jit_solution(12399226877778216470)
XLA Ops:
  0.0 57.2 %exchange.1.messages = s16[32,96,128]{2,1,0:T(8,128)(2,1)} custom-call(bf16[8,512,128]{2,1,0:T(8,128)(2,1)} %duals_hbm.1, bf16[8,128,4096]{2,1,0:T(8,128)(2,1)} %tiles_hbm.1, s32[8,128]{1,0:T(8,128)} %rows_hbm.1, s32[8,128]{1,0:T(8,128)} %cols_hbm.1, s32[8]{0:T(128)} %bitcast.3, f32[8]{0:T(128)} %prob_hbm.1, s32[64]{0:T(128)} %map_hbm.1, f32[40,64,128]{2,1,0:T(8,128)} %bitcast.2), custom_call_target="tpu_custom_call" | custom-call | tf_op jit(solution)/shard_map/exchange/pallas_call | solution.py:364
  57.2 2.6 %finish.1 = f32[2560,128]{1,0:T(8,128)} custom-call(s16[32,96,128]{2,1,0:T(8,128)(2,1)} %exchange.1.messages), custom_call_target="tpu_custom_call" | custom-call | tf_op jit(solution)/shard_map/finish/pallas_call | solution.py:405

commit v6 on v5

--- a/solution.py
+++ b/solution.py
@@ -62,8 +62,7 @@
     stage,
     land,
     selector,
-    high,
-    low,
+    dense,
     weights,
     acc,
     core_in,
@@ -160,16 +159,15 @@
         tiles_copy(s).wait()
         for n in range(WIDE):
             block = tiles_v[s, :, n * 256 : (n + 1) * 256]
-            dense = jnp.dot(selector[...], block, preferred_element_type=jnp.float32)
+            value = jnp.dot(selector[...], block, preferred_element_type=jnp.float32)
             for r in range(nz):
-                part = dense[r * FBD : (r + 1) * FBD]
+                part = value[r * FBD : (r + 1) * FBD]
                 both = jnp.concatenate([part[:, :LANES], part[:, LANES:]], axis=0)
                 upper = both.astype(jnp.bfloat16)
                 lower = (both - upper.astype(jnp.float32)).astype(jnp.bfloat16)
-                high[slot, n * 80 : (n + 1) * 80, r * LANES : (r + 1) * LANES] = upper
-                low[slot, n * 80 : (n + 1) * 80, r * LANES : (r + 1) * LANES] = lower
-
-    densify(0)
+                dense[slot, n * 80 : (n + 1) * 80, r * LANES : (r + 1) * LANES] = upper
+                dense[slot, n * 80 : (n + 1) * 80, (nz + r) * LANES : (nz + r + 1) * LANES] = lower
+
     pl.semaphore_wait(barrier, len(peers))
 
     def z_copy(s, d):
@@ -202,23 +200,12 @@
             z_copy(s, d).start()
         land[s, me] = stage[s, me]
 
-    @pl.loop(1, min(DEEP, scen))
+    @pl.loop(0, min(DEEP, scen))
     def _(s):
         densify(s)
 
-    part = PAIRS // 2
     mine = core * PAIRS
     other = (1 - core) * PAIRS
-
-    def core_copy(k):
-        return pltpu.make_async_remote_copy(
-            src_ref=acc.at[pl.ds(other + k * part, part)],
-            dst_ref=core_in.at[pl.ds(k * part, part)],
-            send_sem=c_send.at[k],
-            recv_sem=c_recv.at[k],
-            device_id=sibling,
-            device_id_type=MESH,
-        )
 
     @pl.loop(0, scen)
     def _(s):
@@ -227,22 +214,15 @@
             z_arrival(s, d).wait_recv()
         for r in range(nz):
             block = land[s, r]
-            weights[r * LANES : r * LANES + TILE, :LANES] = block
-            weights[r * LANES + TILE : (r + 1) * LANES, LANES:] = block
+            for n in (r, nz + r):
+                weights[n * LANES : n * LANES + TILE, :LANES] = block
+                weights[n * LANES + TILE : (n + 1) * LANES, LANES:] = block
 
         scale = prob_ref[s]
-        for n in range(4):
-            rows = slice(n * 320, (n + 1) * 320)
-            value = jnp.dot(high[slot, rows], weights[...], preferred_element_type=jnp.float32)
-            value = value + jnp.dot(low[slot, rows], weights[...], preferred_element_type=jnp.float32)
-            value = value * scale
-            acc[n * 8 : (n + 1) * 8] += value[:, :LANES].reshape(8, FBD, LANES)
-            acc[PAIRS + n * 8 : PAIRS + (n + 1) * 8] += value[:, LANES:].reshape(8, FBD, LANES)
-            if n % 2:
-
-                @pl.when(s == scen - 1)
-                def _():
-                    core_copy(n // 2).start()
+        value = jnp.dot(dense[slot], weights[...], preferred_element_type=jnp.float32)
+        value = value * scale
+        acc[:PAIRS] += value[:, :LANES].reshape(PAIRS, FBD, LANES)
+        acc[PAIRS:] += value[:, LANES:].reshape(PAIRS, FBD, LANES)
 
         @pl.when(s < scen - DEEP)
         def _():
@@ -273,8 +253,9 @@
         return pltpu.make_async_copy(src, out.at[shard], out_sem.at[e])
 
     hops = sorted(range(1, chips), key=lambda e: -min(e // nx, ny - e // nx) - min(e % nx, nx - e % nx))
-    for k in range(2):
-        core_copy(k).wait_recv()
+    core_copy = remote(acc.at[pl.ds(other, PAIRS)], core_in, c_send, c_recv, sibling)
+    core_copy.start()
+    core_copy.wait_recv()
     for first in range(0, chips - 1, GROUP):
         group = hops[first : first + GROUP]
         values = [acc[pl.ds(mine + there(e) * per, per)] + core_in[pl.ds(there(e) * per, per)] for e in group]
@@ -307,8 +288,7 @@
         for d in range(1, nz):
             z_copy(s, d).wait_send()
 
-    for k in range(2):
-        core_copy(k).wait_send()
+    core_copy.wait_send()
     for e in hops:
         r_copy(e).wait_send()
         g_copy(e, core * chips + chip).wait_send()
@@ -377,9 +357,8 @@
             pltpu.VMEM((scen, nz, TILE, LANES), bf16),
             pltpu.VMEM((scen, nz, TILE, LANES), bf16),
             pltpu.VMEM((nz * FBD, SLOTS), bf16),
-            pltpu.VMEM((deep, PAIRS * FBD, nz * LANES), bf16),
-            pltpu.VMEM((deep, PAIRS * FBD, nz * LANES), bf16),
-            pltpu.VMEM((nz * LANES, 2 * LANES), bf16),
+            pltpu.VMEM((deep, PAIRS * FBD, 2 * nz * LANES), bf16),
+            pltpu.VMEM((2 * nz * LANES, 2 * LANES), bf16),
             pltpu.VMEM((TILE, FBD, LANES), f32),
             pltpu.VMEM((PAIRS, FBD, LANES), f32),
             pltpu.VMEM((PAIRS // chips, FBD, LANES), f32),
@@ -392,8 +371,8 @@
             dma((scen,)),
             dma((scen, nz)),
             dma((scen, nz)),
-            dma((2,)),
-            dma((2,)),
+            dma,
+            dma,
         ]
         + [sems] * 6
         + [dma((PAIRS // chips,)), sems],

time: 59.8 us -> 59 us (0.987)
  Pallas kernels: 59.7 us -> 58.9 us
    pallas_call x1, Pallas kernels: 57.2 us -> 56.3 us  [local(): pl.pallas_call(functools.partial(exchange_kernel, ny, nx, nz, scen), out_...]
where the time goes in v6:
time: 59 us; the launch traced here: 58.9 us
  Pallas kernels  58.9 us (100%)
    pallas_call x1, Pallas kernels, local(): pl.pallas_call(functools.partial(exchange_kernel, ny, nx, nz, scen), out_...  56.3 us
    pallas_call x1, Pallas kernels, local(): pl.pallas_call(finish_kernel, out_shape=jax.ShapeDtypeStruct(costs.shape,...  2.58 us

profile of v6, /device:TPU:1, one launch (start us, length us, event | category | flops | bytes accessed | tf_op | source)
XLA Modules:
  0.0 58.9 jit_solution(17092389494962255213)
XLA Ops:
  0.0 56.3 %exchange.1.messages = s16[32,96,128]{2,1,0:T(8,128)(2,1)} custom-call(bf16[8,512,128]{2,1,0:T(8,128)(2,1)} %duals_hbm.1, bf16[8,128,4096]{2,1,0:T(8,128)(2,1)} %tiles_hbm.1, s32[8,128]{1,0:T(8,128)} %rows_hbm.1, s32[8,128]{1,0:T(8,128)} %cols_hbm.1, s32[8]{0:T(128)} %bitcast.3, f32[8]{0:T(128)} %prob_hbm.1, s32[64]{0:T(128)} %map_hbm.1, f32[40,64,128]{2,1,0:T(8,128)} %bitcast.2), custom_call_target="tpu_custom_call" | custom-call | tf_op jit(solution)/shard_map/exchange/pallas_call | solution.py:344
  56.3 2.6 %finish.1 = f32[2560,128]{1,0:T(8,128)} custom-call(s16[32,96,128]{2,1,0:T(8,128)(2,1)} %exchange.1.messages), custom_call_target="tpu_custom_call" | custom-call | tf_op jit(solution)/shard_map/finish/pallas_call | solution.py:384

commit v7 on v6

--- a/solution.py
+++ b/solution.py
@@ -207,9 +207,19 @@
     mine = core * PAIRS
     other = (1 - core) * PAIRS
 
-    @pl.loop(0, scen)
-    def _(s):
-        slot = lax.rem(s, DEEP)
+    part = PAIRS // 2
+
+    def core_copy(k):
+        return pltpu.make_async_remote_copy(
+            src_ref=acc.at[pl.ds(other + k * part, part)],
+            dst_ref=core_in.at[pl.ds(k * part, part)],
+            send_sem=c_send.at[k],
+            recv_sem=c_recv.at[k],
+            device_id=sibling,
+            device_id_type=MESH,
+        )
+
+    def gather_weights(s):
         for d in range(1, nz):
             z_arrival(s, d).wait_recv()
         for r in range(nz):
@@ -218,15 +228,28 @@
                 weights[n * LANES : n * LANES + TILE, :LANES] = block
                 weights[n * LANES + TILE : (n + 1) * LANES, LANES:] = block
 
-        scale = prob_ref[s]
-        value = jnp.dot(dense[slot], weights[...], preferred_element_type=jnp.float32)
-        value = value * scale
-        acc[:PAIRS] += value[:, :LANES].reshape(PAIRS, FBD, LANES)
-        acc[PAIRS:] += value[:, LANES:].reshape(PAIRS, FBD, LANES)
+    def multiply(s, start, count):
+        rows = slice(start * FBD, (start + count) * FBD)
+        value = jnp.dot(dense[s % DEEP if isinstance(s, int) else lax.rem(s, DEEP), rows], weights[...], preferred_element_type=jnp.float32)
+        value = value * prob_ref[s]
+        acc[start : start + count] += value[:, :LANES].reshape(count, FBD, LANES)
+        acc[PAIRS + start : PAIRS + start + count] += value[:, LANES:].reshape(count, FBD, LANES)
+
+    @pl.loop(0, scen - 1)
+    def _(s):
+        gather_weights(s)
+        multiply(s, 0, PAIRS)
 
         @pl.when(s < scen - DEEP)
         def _():
             densify(s + DEEP)
+
+    final = scen - 1
+    gather_weights(final)
+    for k in range(2):
+        multiply(final, k * part, part // 2)
+        multiply(final, k * part + part // 2, part // 2)
+        core_copy(k).start()
 
     def remote(src, dst, send, recv, to):
         return pltpu.make_async_remote_copy(
@@ -253,9 +276,8 @@
         return pltpu.make_async_copy(src, out.at[shard], out_sem.at[e])
 
     hops = sorted(range(1, chips), key=lambda e: -min(e // nx, ny - e // nx) - min(e % nx, nx - e % nx))
-    core_copy = remote(acc.at[pl.ds(other, PAIRS)], core_in, c_send, c_recv, sibling)
-    core_copy.start()
-    core_copy.wait_recv()
+    for k in range(2):
+        core_copy(k).wait_recv()
     for first in range(0, chips - 1, GROUP):
         group = hops[first : first + GROUP]
         values = [acc[pl.ds(mine + there(e) * per, per)] + core_in[pl.ds(there(e) * per, per)] for e in group]
@@ -288,7 +310,8 @@
         for d in range(1, nz):
             z_copy(s, d).wait_send()
 
-    core_copy.wait_send()
+    for k in range(2):
+        core_copy(k).wait_send()
     for e in hops:
         r_copy(e).wait_send()
         g_copy(e, core * chips + chip).wait_send()
@@ -371,8 +394,8 @@
             dma((scen,)),
             dma((scen, nz)),
             dma((scen, nz)),
-            dma,
-            dma,
+            dma((2,)),
+            dma((2,)),
         ]
         + [sems] * 6
         + [dma((PAIRS // chips,)), sems],

time: 59 us -> 58.6 us (level)
  no operation moved by 1% of the time
where the time goes in v7:
time: 58.6 us; the launch traced here: 58.5 us
  Pallas kernels  58.5 us (100%)
    pallas_call x1, Pallas kernels, local(): pl.pallas_call(functools.partial(exchange_kernel, ny, nx, nz, scen), out_...  55.9 us
    pallas_call x1, Pallas kernels, local(): pl.pallas_call(finish_kernel, out_shape=jax.ShapeDtypeStruct(costs.shape,...  2.58 us

profile of v7, /device:TPU:1, one launch (start us, length us, event | category | flops | bytes accessed | tf_op | source)
XLA Modules:
  0.0 58.5 jit_solution(5772081317167352705)
XLA Ops:
  0.0 55.9 %exchange.1.messages = s16[32,96,128]{2,1,0:T(8,128)(2,1)} custom-call(bf16[8,512,128]{2,1,0:T(8,128)(2,1)} %duals_hbm.1, bf16[8,128,4096]{2,1,0:T(8,128)(2,1)} %tiles_hbm.1, s32[8,128]{1,0:T(8,128)} %rows_hbm.1, s32[8,128]{1,0:T(8,128)} %cols_hbm.1, s32[8]{0:T(128)} %bitcast.3, f32[8]{0:T(128)} %prob_hbm.1, s32[64]{0:T(128)} %map_hbm.1, f32[40,64,128]{2,1,0:T(8,128)} %bitcast.2), custom_call_target="tpu_custom_call" | custom-call | tf_op jit(solution)/shard_map/exchange/pallas_call | solution.py:367
  55.9 2.6 %finish.1 = f32[2560,128]{1,0:T(8,128)} custom-call(s16[32,96,128]{2,1,0:T(8,128)(2,1)} %exchange.1.messages), custom_call_target="tpu_custom_call" | custom-call | tf_op jit(solution)/shard_map/finish/pallas_call | solution.py:407

commit v8 on v7

--- a/solution.py
+++ b/solution.py
@@ -411,7 +411,7 @@
         out_specs=hbm,
         scratch_shapes=[
             pltpu.VMEM(messages.shape, i16),
-            pltpu.VMEM(costs.shape, f32),
+            pltpu.VMEM((costs.shape[0] + TILE, LANES), f32),
             dma((FBD // 8 + 1,)),
             dma((FBD // 8,)),
         ],

time: 58.6 us -> 58.6 us (level)
  no operation moved by 1% of the time
where the time goes in v8:
time: 58.6 us; the launch traced here: 58.5 us
  Pallas kernels  58.5 us (100%)
    pallas_call x1, Pallas kernels, local(): pl.pallas_call(functools.partial(exchange_kernel, ny, nx, nz, scen), out_...  55.9 us
    pallas_call x1, Pallas kernels, local(): pl.pallas_call(finish_kernel, out_shape=jax.ShapeDtypeStruct(costs.shape,...  2.58 us

profile of v8, /device:TPU:1, one launch (start us, length us, event | category | flops | bytes accessed | tf_op | source)
XLA Modules:
  0.0 58.5 jit_solution(5772081317167352705)
XLA Ops:
  0.0 55.9 %exchange.1.messages = s16[32,96,128]{2,1,0:T(8,128)(2,1)} custom-call(bf16[8,512,128]{2,1,0:T(8,128)(2,1)} %duals_hbm.1, bf16[8,128,4096]{2,1,0:T(8,128)(2,1)} %tiles_hbm.1, s32[8,128]{1,0:T(8,128)} %rows_hbm.1, s32[8,128]{1,0:T(8,128)} %cols_hbm.1, s32[8]{0:T(128)} %bitcast.3, f32[8]{0:T(128)} %prob_hbm.1, s32[64]{0:T(128)} %map_hbm.1, f32[40,64,128]{2,1,0:T(8,128)} %bitcast.2), custom_call_target="tpu_custom_call" | custom-call | tf_op jit(solution)/shard_map/exchange/pallas_call | solution.py:367
  55.9 2.6 %finish.1 = f32[2560,128]{1,0:T(8,128)} custom-call(s16[32,96,128]{2,1,0:T(8,128)(2,1)} %exchange.1.messages), custom_call_target="tpu_custom_call" | custom-call | tf_op jit(solution)/shard_map/finish/pallas_call | solution.py:407
